TPU v7x, 32 devices: a whole 2x2x4 slice. The times are simulated.
32 devices in a mesh: batch: 8 (over y, x, core), ctx: 4 (over z).
Axes of the slice: x: 2, y: 2, z: 4, core: 2. Of those that a mesh axis runs over, the one named last changes fastest.
Arguments:
- block_in: bfloat16 [8, 8, 128, 768], P('batch', 'ctx'), may hold values from -6 to 6
- cotangent: bfloat16 [8, 8, 128, 768], P('batch', 'ctx'), may hold values from -6 to 6
- w_qkv: float32 [768, 2304], P('batch', 'ctx'), may hold values from -0.21875 to 0.21875
- w_out: float32 [768, 768], P('batch', 'ctx'), may hold values from -0.875 to 0.875
- w_fc: float32 [768, 3072], P('batch', 'ctx'), may hold values from -0.21875 to 0.21875
- w_proj: float32 [3072, 768], P('batch', 'ctx'), may hold values from -0.109375 to 0.109375
- vectors: float32 [12, 768], P(None, 'ctx'), may hold values from -0.5 to 1.5, as said below
- qkv_first: float32 [768, 2304], P('batch', 'ctx'), may hold values from -16 to 16
- qkv_second: float32 [768, 2304], P('batch', 'ctx'), may hold values from 0.73728 to 2.94912
- out_first: float32 [768, 768], P('batch', 'ctx'), may hold values from -28 to 28
- out_second: float32 [768, 768], P('batch', 'ctx'), may hold values from 2.048 to 8.192
- fc_first: float32 [768, 3072], P('batch', 'ctx'), may hold values from -28 to 28
- fc_second: float32 [768, 3072], P('batch', 'ctx'), may hold values from 2.048 to 8.192
- proj_first: float32 [3072, 768], P('batch', 'ctx'), may hold values from -28 to 28
- proj_second: float32 [3072, 768], P('batch', 'ctx'), may hold values from 2.048 to 8.192
- vec_first: float32 [12, 768], P(None, 'ctx'), may hold values from -56 to 56
- vec_second: float32 [12, 768], P(None, 'ctx'), may hold values from 8.192 to 32.768
Outputs:
- out_block: bfloat16 [8, 8, 128, 768], P('batch', 'ctx')
- grad_input: float32 [8, 8, 128, 768], P('batch', 'ctx')
- qkv_first_new: float32 [768, 2304], P('batch', 'ctx')
- qkv_second_new: float32 [768, 2304], P('batch', 'ctx')
- qkv_new: float32 [768, 2304], P('batch', 'ctx')
- out_first_new: float32 [768, 768], P('batch', 'ctx')
- out_second_new: float32 [768, 768], P('batch', 'ctx')
- out_new: float32 [768, 768], P('batch', 'ctx')
- fc_first_new: float32 [768, 3072], P('batch', 'ctx')
- fc_second_new: float32 [768, 3072], P('batch', 'ctx')
- fc_new: float32 [768, 3072], P('batch', 'ctx')
- proj_first_new: float32 [3072, 768], P('batch', 'ctx')
- proj_second_new: float32 [3072, 768], P('batch', 'ctx')
- proj_new: float32 [3072, 768], P('batch', 'ctx')
- vec_first_new: float32 [12, 768], P(None, 'ctx')
- vec_second_new: float32 [12, 768], P(None, 'ctx')
- vec_new: float32 [12, 768], P(None, 'ctx')
Inputs may be any that keep to these rules, and one draw needn't show every extreme that they name: `vectors`: rows 0 and 2 are gains between 0.5 and 1.5; the other rows are biases between -0.5 and 0.5.
All inputs are finite; a program needn't handle non-finite values.
Results may differ from a plain program's by a relative error of at most 0.0085.
The roundings to bfloat16 on the way count: a program that leaves them out, or rounds other values in their place, can miss the bound.
Values may be sent and summed in bfloat16 or wider, within the bound.
No kernel may reach another device: no remote copies, remote signals or barrier semaphores. Data moves between devices by JAX's collectives and lax.ppermute only.
A program may use at most 128 MiB of HBM per device.

v0:
```python
import functools
import math

import jax
import jax.numpy as jnp
from jax import lax
from jax.experimental import pallas as pl
from jax.experimental.pallas import tpu as pltpu
from jax.sharding import PartitionSpec as P

HEADS = 12
STEP = 10


def layer_norm(value, gain, shift):
    mean = jnp.mean(value, axis=-1, keepdims=True)
    centred = value - mean
    spread = jnp.mean(centred * centred, axis=-1, keepdims=True)
    return centred * lax.rsqrt(spread + 1e-05) * gain + shift


def gelu_tanh(value):
    return (
        0.5
        * value
        * (1.0 + jnp.tanh(0.7978845608028654 * (value + 0.044715 * value * value * value)))
    )


def block_places(index, count, half):
    offsets = jnp.arange(half, dtype=jnp.int32)
    first = index * half + offsets
    second = (2 * count - 1 - index) * half + offsets
    return jnp.concatenate([first, second])


def scores_of(queries, keys, scale, allowed):
    raw = jnp.einsum("sqhd,skhd->shqk", queries, keys, preferred_element_type=jnp.float32) * scale
    return jnp.where(allowed[None, None], raw, -1e30)


def pair_grads(queries, grads, keys, values, top, total, delta, scale, allowed):
    score = scores_of(queries, keys, scale, allowed)
    weights = jnp.exp(score - top[..., None]) / total[..., None]
    back_weights = jnp.einsum("sqhd,skhd->shqk", grads, values, preferred_element_type=jnp.float32)
    grad_score = (weights * (back_weights - delta[..., None])).astype(jnp.bfloat16)
    return (weights.astype(jnp.bfloat16), grad_score)


def rows_product(left, right):
    return jnp.einsum("ra,rb->ab", left, right, preferred_element_type=jnp.float32)


def back_product(grad, weight):
    return jnp.einsum("rb,ab->ra", grad, weight, preferred_element_type=jnp.float32)


def adamw(weight, grad, first, second, rate, decay):
    first = 0.9 * first + 0.1 * grad
    second = 0.999 * second + 0.001 * grad * grad
    first_hat = first / (1.0 - 0.9**STEP)
    second_hat = second / (1.0 - 0.999**STEP)
    weight = weight - rate * (first_hat / (jnp.sqrt(second_hat) + 1e-08) + decay * weight)
    return (first, second, weight)


def local_any(
    block_in,
    cotangent,
    w_qkv,
    w_out,
    w_fc,
    w_proj,
    vectors,
    qkv_first,
    qkv_second,
    out_first,
    out_second,
    fc_first,
    fc_second,
    proj_first,
    proj_second,
    vec_first,
    vec_second,
):
    low_type = jnp.bfloat16
    wide = jnp.float32
    row_parts = (
        lax.all_gather(w_qkv.astype(low_type), "batch", axis=0, tiled=True),
        lax.all_gather(w_out.astype(low_type), "batch", axis=0, tiled=True),
        lax.all_gather(w_fc.astype(low_type), "batch", axis=0, tiled=True),
        lax.all_gather(w_proj.astype(low_type), "batch", axis=0, tiled=True),
    )
    full_qkv, full_out, full_fc, full_proj, full_vec = (
        lax.all_gather(row_parts[0], "ctx", axis=1, tiled=True),
        lax.all_gather(row_parts[1], "ctx", axis=1, tiled=True),
        lax.all_gather(row_parts[2], "ctx", axis=1, tiled=True),
        lax.all_gather(row_parts[3], "ctx", axis=1, tiled=True),
        lax.all_gather(vectors.astype(low_type), "ctx", axis=1, tiled=True),
    )
    params = full_vec.astype(wide)
    seqs, pair, half, width = block_in.shape
    heads = HEADS
    head = width // heads
    rows = seqs * pair * half
    span = pair * half
    count = lax.axis_size("ctx")
    index = lax.axis_index("ctx")
    scale = 1.0 / math.sqrt(head)
    inputs = block_in.astype(wide).reshape(rows, width)
    normed_one = layer_norm(inputs, params[0], params[1]).astype(low_type)
    mixed = jnp.dot(normed_one, full_qkv, preferred_element_type=wide)
    queries = (mixed[:, :width] + params[4]).astype(low_type)
    keys = mixed[:, width : 2 * width].astype(low_type)
    values = (mixed[:, 2 * width :] + params[5]).astype(low_type)
    key_all, value_all = (
        lax.all_gather(keys.reshape(seqs, pair, half, width), "ctx", axis=1, tiled=True),
        lax.all_gather(values.reshape(seqs, pair, half, width), "ctx", axis=1, tiled=True),
    )
    query_heads = queries.reshape(seqs, span, heads, head)
    own_places = block_places(index, count, half)

    def piece_of(source, piece):
        return lax.dynamic_slice_in_dim(source, 2 * piece, 2, 1).reshape(seqs, span, heads, head)

    def allowed_for(piece):
        return own_places[:, None] >= block_places(piece, count, half)[None, :]

    def stats_step(piece, carry):
        top, total = carry
        score = scores_of(query_heads, piece_of(key_all, piece), scale, allowed_for(piece))
        new_top = jnp.maximum(top, jnp.max(score, axis=-1))
        total = total * jnp.exp(top - new_top) + jnp.sum(
            jnp.exp(score - new_top[..., None]), axis=-1
        )
        return (new_top, total)

    start_stats = (jnp.full((seqs, heads, span), -1e30, wide), jnp.zeros((seqs, heads, span), wide))
    top, total = lax.fori_loop(0, count, stats_step, start_stats)

    def output_step(piece, acc):
        score = scores_of(query_heads, piece_of(key_all, piece), scale, allowed_for(piece))
        weights = (jnp.exp(score - top[..., None]) / total[..., None]).astype(low_type)
        return acc + jnp.einsum(
            "shqk,skhd->sqhd", weights, piece_of(value_all, piece), preferred_element_type=wide
        )

    attended = lax.fori_loop(0, count, output_step, jnp.zeros((seqs, span, heads, head), wide))
    att_low = attended.reshape(rows, width).astype(low_type)
    mid = inputs + jnp.dot(att_low, full_out, preferred_element_type=wide) + params[6]
    normed_two = layer_norm(mid, params[2], params[3]).astype(low_type)
    pre = jnp.dot(normed_two, full_fc, preferred_element_type=wide) + params[8:12].reshape(-1)
    act_low = gelu_tanh(pre).astype(low_type)
    result = mid + jnp.dot(act_low, full_proj, preferred_element_type=wide) + params[7]
    out_block = result.astype(low_type).reshape(block_in.shape)
    grad_low = cotangent.reshape(rows, width)
    grad_out = grad_low.astype(wide)
    grad_wproj = rows_product(act_low, grad_low)
    back_act = back_product(grad_low, full_proj)
    grad_pre = jax.vjp(gelu_tanh, pre)[1](back_act)[0].astype(low_type)
    grad_wfc = rows_product(normed_two, grad_pre)
    back_two = back_product(grad_pre, full_fc)
    back_mid, grad_gain_two, grad_shift_two = jax.vjp(layer_norm, mid, params[2], params[3])[1](
        back_two
    )
    grad_mid = grad_out + back_mid
    grad_att_low = grad_mid.astype(low_type)
    grad_wout = rows_product(att_low, grad_att_low)
    back_att = back_product(grad_att_low, full_out)
    grad_heads = back_att.astype(low_type).reshape(seqs, span, heads, head)
    delta = jnp.einsum("sqhd,sqhd->shq", grad_heads.astype(wide), attended)
    query_all, grad_all = (
        lax.all_gather(queries.reshape(seqs, pair, half, width), "ctx", axis=1, tiled=True),
        lax.all_gather(grad_heads.reshape(seqs, pair, half, width), "ctx", axis=1, tiled=True),
    )
    top_all, total_all, delta_all = (
        lax.all_gather(top.reshape(seqs, heads, pair, half), "ctx", axis=2, tiled=True),
        lax.all_gather(total.reshape(seqs, heads, pair, half), "ctx", axis=2, tiled=True),
        lax.all_gather(delta.reshape(seqs, heads, pair, half), "ctx", axis=2, tiled=True),
    )

    def query_step(piece, grad_query):
        key_part = piece_of(key_all, piece)
        value_part = piece_of(value_all, piece)
        weights_low, grad_score = pair_grads(
            query_heads,
            grad_heads,
            key_part,
            value_part,
            top,
            total,
            delta,
            scale,
            allowed_for(piece),
        )
        return grad_query + jnp.einsum(
            "shqk,skhd->sqhd", grad_score, key_part, preferred_element_type=wide
        )

    grad_query = lax.fori_loop(0, count, query_step, jnp.zeros((seqs, span, heads, head), wide))
    key_heads = keys.reshape(seqs, span, heads, head)
    value_heads = values.reshape(seqs, span, heads, head)

    def stat_piece(source, piece):
        return lax.dynamic_slice_in_dim(source, 2 * piece, 2, 2).reshape(seqs, heads, span)

    def key_step(piece, carry):
        grad_key, grad_value = carry
        query_part = piece_of(query_all, piece)
        grad_part = piece_of(grad_all, piece)
        allowed = block_places(piece, count, half)[:, None] >= own_places[None, :]
        weights_low, grad_score = pair_grads(
            query_part,
            grad_part,
            key_heads,
            value_heads,
            stat_piece(top_all, piece),
            stat_piece(total_all, piece),
            stat_piece(delta_all, piece),
            scale,
            allowed,
        )
        grad_key = grad_key + jnp.einsum(
            "shqk,sqhd->skhd", grad_score, query_part, preferred_element_type=wide
        )
        grad_value = grad_value + jnp.einsum(
            "shqk,sqhd->skhd", weights_low, grad_part, preferred_element_type=wide
        )
        return (grad_key, grad_value)

    start_keys = (
        jnp.zeros((seqs, span, heads, head), wide),
        jnp.zeros((seqs, span, heads, head), wide),
    )
    grad_key, grad_value = lax.fori_loop(0, count, key_step, start_keys)
    grad_keys = (grad_key * scale).reshape(seqs, pair, half, width)
    grad_values = grad_value.reshape(seqs, pair, half, width)
    grad_q_low = (grad_query * scale).reshape(rows, width).astype(low_type)
    grad_k_low = grad_keys.reshape(rows, width).astype(low_type)
    grad_v_low = grad_values.reshape(rows, width).astype(low_type)
    grad_mixed = jnp.concatenate([grad_q_low, grad_k_low, grad_v_low], axis=1)
    grad_wqkv = rows_product(normed_one, grad_mixed)
    back_one = back_product(grad_mixed, full_qkv)
    back_in, grad_gain_one, grad_shift_one = jax.vjp(layer_norm, inputs, params[0], params[1])[1](
        back_one
    )
    grad_input = (grad_mid + back_in).reshape(block_in.shape)
    grad_bias_q = jnp.sum(grad_q_low.astype(wide), axis=0)
    grad_bias_v = jnp.sum(grad_v_low.astype(wide), axis=0)
    grad_bias_out = jnp.sum(grad_att_low.astype(wide), axis=0)
    grad_bias_proj = jnp.sum(grad_out, axis=0)
    grad_bias_fc = jnp.sum(grad_pre.astype(wide), axis=0).reshape(4, width)
    small_rows = jnp.stack(
        [
            grad_gain_one,
            grad_shift_one,
            grad_gain_two,
            grad_shift_two,
            grad_bias_q,
            grad_bias_v,
            grad_bias_out,
            grad_bias_proj,
        ]
    )
    grad_vectors = jnp.concatenate([small_rows, grad_bias_fc], axis=0)
    col_sums = (
        lax.psum_scatter(grad_wqkv, "ctx", scatter_dimension=1, tiled=True),
        lax.psum_scatter(grad_wout, "ctx", scatter_dimension=1, tiled=True),
        lax.psum_scatter(grad_wfc, "ctx", scatter_dimension=1, tiled=True),
        lax.psum_scatter(grad_wproj, "ctx", scatter_dimension=1, tiled=True),
        lax.psum_scatter(grad_vectors, "ctx", scatter_dimension=1, tiled=True),
    )
    qkv_grad, out_grad, fc_grad, proj_grad = (
        lax.psum_scatter(col_sums[0], "batch", scatter_dimension=0, tiled=True),
        lax.psum_scatter(col_sums[1], "batch", scatter_dimension=0, tiled=True),
        lax.psum_scatter(col_sums[2], "batch", scatter_dimension=0, tiled=True),
        lax.psum_scatter(col_sums[3], "batch", scatter_dimension=0, tiled=True),
    )
    vec_grad = lax.psum(col_sums[4], "batch")
    qkv_m, qkv_s, qkv_w = adamw(w_qkv, qkv_grad, qkv_first, qkv_second, 0.06, 0.1)
    out_m, out_s, out_w = adamw(w_out, out_grad, out_first, out_second, 0.06, 0.1)
    fc_m, fc_s, fc_w = adamw(w_fc, fc_grad, fc_first, fc_second, 0.06, 0.1)
    proj_m, proj_s, proj_w = adamw(w_proj, proj_grad, proj_first, proj_second, 0.06, 0.1)
    vec_m, vec_s, vec_w = adamw(vectors, vec_grad, vec_first, vec_second, 0.2, 0.0)
    return (
        out_block,
        grad_input,
        qkv_m,
        qkv_s,
        qkv_w,
        out_m,
        out_s,
        out_w,
        fc_m,
        fc_s,
        fc_w,
        proj_m,
        proj_s,
        proj_w,
        vec_m,
        vec_s,
        vec_w,
    )


BATCH = 8
CTX = 4
WIDTH = 768
HEAD = 64
GROUP = WIDTH // CTX
TOKENS = 256
HALF = 128
FF_SIDE = 384
ROWS = WIDTH // BATCH
MLP = WIDTH + 2 * FF_SIDE + 256
SPAN = TOKENS * CTX
TILE = 256
LOW = jnp.bfloat16
WIDE = jnp.float32
CORE, XBIT, YBIT = 1, 2, 4
PLACES = (0, 1, 2, 3)
DIFFERENCES = (0, 2, 1, 3)
SOURCES = (
    (0, PLACES),
    (XBIT, PLACES),
    (YBIT, PLACES),
    (XBIT + YBIT, PLACES[:2]),
    (XBIT + YBIT, PLACES[2:]),
    (CORE, PLACES),
    (CORE + XBIT, PLACES),
    (CORE + YBIT, PLACES),
    (CORE + XBIT + YBIT, PLACES[:2]),
    (CORE + XBIT + YBIT, PLACES[2:]),
)
PARTS = len(SOURCES)
VMEM_LIMIT = 56 * 1024 * 1024


def swap(value, axis, bit):
    size = BATCH if axis == "batch" else CTX
    return lax.ppermute(value, axis, [(i, i ^ bit) for i in range(size)])


def mm(left, right):
    return lax.dot_general(left, right, (((1,), (0,)), ((), ())), preferred_element_type=WIDE)


def mt(left, right):
    return lax.dot_general(left, right, (((1,), (1,)), ((), ())), preferred_element_type=WIDE)


def tm(left, right):
    return lax.dot_general(left, right, (((0,), (0,)), ((), ())), preferred_element_type=WIDE)


def turned(value):
    return value.astype(WIDE).T.astype(LOW)


def moments(value):
    mean = jnp.mean(value, axis=-1, keepdims=True)
    centred = value - mean
    spread = jnp.mean(centred * centred, axis=-1, keepdims=True)
    return centred, lax.rsqrt(spread + 1e-05)


def norm_back(grad, normed, inverse, gain):
    part = grad * gain
    mean = jnp.mean(part, axis=-1, keepdims=True)
    cross = jnp.mean(part * normed, axis=-1, keepdims=True)
    return inverse * (part - mean - normed * cross)


def exchange(value):
    return swap(value, "ctx", 1), swap(value, "ctx", 2), swap(value, "ctx", 3)


def gather_first(own):
    return swap(own, "batch", XBIT), swap(own, "batch", YBIT)


def gather_second(from_x, from_y):
    return swap(from_x[:2], "batch", YBIT), swap(from_y[2:], "batch", XBIT)


def to_core(parts):
    return [swap(part, "batch", CORE) for part in parts]


def swap_pair(pair, first, second):
    return swap(pair[0], "batch", first), swap(pair[1], "batch", second)


def scatter_second(kept, back):
    one = kept[0].astype(WIDE) + back[0].astype(WIDE)
    two = kept[1].astype(WIDE) + back[1].astype(WIDE)
    return (one[0], two[0]), (one[1].astype(LOW), two[1].astype(LOW))


def scatter_near(kept, back):
    one = kept[0].astype(WIDE) + back[0].astype(WIDE)
    two = (kept[1].astype(WIDE) + back[1].astype(WIDE)).astype(LOW)
    return one, swap(two, "ctx", 1)


def scatter_far(one, two):
    one = one + two.astype(WIDE)
    return one[0] + swap(one[1].astype(LOW), "ctx", 2).astype(WIDE)


def rows_of(index, size):
    return pl.ds(pl.multiple_of(index * size, 16), size)


def qkv_place(held, batch, ctx):
    return [(pl.ds(0, 3 * GROUP), held.at[ctx, rows_of(batch, ROWS), :])]


def mlp_place(held_out, held_fc, held_proj, batch, ctx):
    return [
        (pl.ds(WIDTH + 2 * FF_SIDE, TILE), held_out.at[ctx, rows_of(batch, ROWS), :]),
        (pl.ds(0, WIDTH), held_fc.at[ctx, rows_of(batch, ROWS), :]),
        (pl.ds(WIDTH, FF_SIDE), held_proj.at[batch, rows_of(2 * ctx, ROWS), :]),
        (pl.ds(WIDTH + FF_SIDE, FF_SIDE), held_proj.at[batch, rows_of(2 * ctx + 1, ROWS), :]),
    ]


def load_weight(meta, parts, place, sems, shift):
    copies = []
    for part, (source, places) in zip(parts, SOURCES):
        for index, ctx in enumerate(places):
            ranges = place(meta[0] ^ source, shift ^ ctx)
            copies.append([(part.at[index, :, lanes], target) for lanes, target in ranges])
    started = []
    for kind in range(len(copies[0])):
        group = []
        for number, copy in enumerate(copies):
            group.append(pltpu.make_async_copy(*copy[kind], sems.at[kind, number]))
            group[-1].start()
        started.append(group)
    return started


def store_grad(held, targets, sems):
    one_kept, one_sent, two_kept, two_sent = targets
    copies = []
    for y in range(2):
        for x in range(2):
            for index, ctx in enumerate(DIFFERENCES):
                if index < 2:
                    target = (one_sent if y else one_kept).at[x, index]
                else:
                    target = (two_sent if x else two_kept).at[y, index - 2]
                for kind, (lanes, source) in enumerate(held(2 * y + x, ctx)):
                    number = (2 * y + x) * CTX + ctx
                    copies.append(
                        pltpu.make_async_copy(source, target.at[:, lanes], sems.at[kind, number])
                    )
                    copies[-1].start()
    wait_all(copies)


def half_rows(meta, pair, held):
    for index, value in enumerate(pair):
        held[index] = turned(value)
    parts = []
    for index in range(2):
        rows = [held[index, rows_of(meta[0] ^ (2 * part), ROWS), :] for part in range(BATCH // 2)]
        parts.append(jnp.concatenate(rows, axis=0))
    return parts


def over_both(left, right):
    return mm(left[0], right[0]) + mm(left[1], right[1])


def wait_all(copies):
    for copy in copies:
        copy.wait()


LANES = 128


def write_packed(target, value):
    full = value.shape[1] // LANES
    for index in range(full):
        target[index * TOKENS : (index + 1) * TOKENS, :] = value[
            :, index * LANES : (index + 1) * LANES
        ]
    rest = value[:, full * LANES :]
    target[full * TOKENS :, :] = jnp.concatenate([rest[:HALF], rest[HALF:]], axis=1)


def read_packed(source):
    full = source.shape[0] // TOKENS
    parts = [source[index * TOKENS : (index + 1) * TOKENS, :] for index in range(full)]
    rest = source[full * TOKENS :, :]
    parts.append(jnp.concatenate([rest[:, : LANES // 2], rest[:, LANES // 2 :]], axis=0))
    return jnp.concatenate(parts, axis=1)


def in_place(ctx, block):
    first = ctx if block == 0 else 2 * CTX - 1 - ctx
    return pl.ds(pl.multiple_of(first * HALF, HALF), HALF)


def read_vectors(meta, parts, chunks):
    for ctx, part in enumerate(parts):
        rows = [part[16 * index : 16 * (index + 1), :] for index in range(GROUP // HEAD)]
        chunks[meta[1] ^ ctx] = jnp.concatenate(rows, axis=1).astype(WIDE)
    return jnp.concatenate([chunks[index] for index in range(CTX)], axis=1)


def qkv_kernel(meta, x_ref, *refs):
    vectors, parts, refs = refs[:4], refs[4 : 4 + PARTS], refs[4 + PARTS :]
    h_ref, own, near, far, last, held, units, chunks, sems = refs
    (copies,) = load_weight(meta, parts, functools.partial(qkv_place, held), sems, meta[1])
    params = read_vectors(meta, vectors, chunks)
    bias = jnp.concatenate([params[4:5], jnp.zeros((1, WIDTH), WIDE), params[5:6]], axis=1)
    centred, inverse = moments(x_ref[...].astype(WIDE))
    normed = (centred * inverse * params[0:1] + params[1:2]).astype(LOW)
    h_ref[...] = normed
    wait_all(copies)
    for chunk in range(CTX):
        mixed = mm(normed, held[chunk]) + bias[:, 3 * GROUP * chunk : 3 * GROUP * (chunk + 1)]
        mixed = mixed.astype(LOW)
        for part in range(3):
            unit = 3 * chunk + part
            units[unit % CTX, :, (unit // CTX) * GROUP : (unit // CTX + 1) * GROUP] = mixed[
                :, part * GROUP : (part + 1) * GROUP
            ]
    for ctx, target in enumerate((own, near, far, last)):
        write_packed(target, units[meta[1] ^ ctx])


def read_sequence(meta, pieces, targets):
    for ctx, piece in enumerate(pieces):
        value = read_packed(piece)
        for block in range(2):
            place = in_place(meta[1] ^ ctx, block)
            rows = value[block * HALF : (block + 1) * HALF, :]
            for index, target in enumerate(targets):
                target[place, :] = rows[:, index * GROUP : (index + 1) * GROUP]


def write_sequence(meta, pieces, sources):
    for ctx, piece in enumerate(pieces):
        parts = []
        for source in sources:
            blocks = [source[in_place(meta[1] ^ ctx, block), :] for block in range(2)]
            parts.append(jnp.concatenate(blocks, axis=0).astype(LOW))
        write_packed(piece, jnp.concatenate(parts, axis=1))


def head_mask(head, scale=1.0):
    lane = lax.broadcasted_iota(jnp.int32, (1, GROUP), 1)
    inside = (lane >= head * HEAD) & (lane < (head + 1) * HEAD)
    return jnp.where(inside, scale, 0.0).astype(LOW)


def tile_of(index):
    return slice(index * TILE, (index + 1) * TILE)


def weights_of(queries, k_seq, tile, causal):
    scores = [mt(queries, k_seq[tile_of(other), :]) for other in range(tile + 1)]
    scores[tile] = jnp.where(causal, scores[tile], -1e30)
    top = jnp.max(functools.reduce(jnp.maximum, scores), axis=-1, keepdims=True)
    expo = [jnp.exp(score - top) for score in scores]
    total = jnp.sum(functools.reduce(jnp.add, expo), axis=-1, keepdims=True)
    inverse = 1.0 / total
    return [value * inverse for value in expo]


def causal_tile():
    row = lax.broadcasted_iota(jnp.int32, (TILE, TILE), 0)
    column = lax.broadcasted_iota(jnp.int32, (TILE, TILE), 1)
    return row >= column


def attend_kernel(meta, *refs):
    pieces, results, (q_seq, k_seq, v_seq, out) = refs[:4], refs[4:8], refs[8:]
    read_sequence(meta, pieces, (q_seq, k_seq, v_seq))
    causal = causal_tile()
    scale = 1.0 / math.sqrt(HEAD)
    for tile in range(SPAN // TILE):

        def one_head(head, total, tile=tile):
            mask = head_mask(head)
            queries = q_seq[tile_of(tile), :] * head_mask(head, scale)
            weights = weights_of(queries, k_seq, tile, causal)
            for other, weight in enumerate(weights):
                total = total + mm(weight.astype(LOW), v_seq[tile_of(other), :] * mask)
            return total

        out[tile_of(tile), :] = lax.fori_loop(
            0, GROUP // HEAD, one_head, jnp.zeros((TILE, GROUP), WIDE), unroll=True
        )
    write_sequence(meta, results, (out,))


def attend_back_kernel(meta, *refs):
    pieces, grads, results = refs[:4], refs[4:8], refs[8:12]
    q_seq, k_seq, v_seq, g_seq, dq, dk, dv = refs[12:]
    read_sequence(meta, pieces, (q_seq, k_seq, v_seq))
    read_sequence(meta, grads, (g_seq,))
    causal = causal_tile()
    scale = 1.0 / math.sqrt(HEAD)
    dk[...] = jnp.zeros_like(dk)
    dv[...] = jnp.zeros_like(dv)
    for tile in range(SPAN // TILE):

        def one_head(head, total, tile=tile):
            mask = head_mask(head)
            scaled = head_mask(head, scale)
            queries = q_seq[tile_of(tile), :] * scaled
            grad = g_seq[tile_of(tile), :] * mask
            weights = weights_of(queries, k_seq, tile, causal)
            backs = [mt(grad, v_seq[tile_of(other), :]) for other in range(tile + 1)]
            products = [weight * back for weight, back in zip(weights, backs)]
            delta = jnp.sum(functools.reduce(jnp.add, products), axis=-1, keepdims=True)
            for other, (weight, back) in enumerate(zip(weights, backs)):
                step = (weight * (back - delta)).astype(LOW)
                total = total + mm(step, k_seq[tile_of(other), :] * scaled)
                dk[tile_of(other), :] += tm(step, queries)
                dv[tile_of(other), :] += tm(weight.astype(LOW), grad)
            return total

        dq[tile_of(tile), :] = lax.fori_loop(
            0, GROUP // HEAD, one_head, jnp.zeros((TILE, GROUP), WIDE), unroll=True
        )
    write_sequence(meta, results, (dq, dk, dv))


def middle_kernel(meta, x_ref, dy_ref, h_one_ref, *refs):
    vectors, pieces, parts, refs = refs[:4], refs[4:8], refs[8 : 8 + PARTS], refs[8 + PARTS :]
    (out_ref, pack_ref, mine, theirs, dmid_ref), refs = refs[:5], refs[5:]
    results, (rows_ref, dbias_ref), refs = refs[:4], refs[4:6], refs[6:]
    out_parts, held_out, held_fc, held_proj, units, total, back, chunks, bias, acts, sems = refs
    place = functools.partial(mlp_place, out_parts, held_fc, held_proj)
    copies = load_weight(meta, parts, place, sems, 0)
    vec = read_vectors(meta, vectors, chunks)
    for chunk in range(CTX):
        bias[chunk] = vec[8 + chunk : 9 + chunk]
    for ctx, piece in enumerate(pieces):
        units[meta[1] ^ ctx] = read_packed(piece)
    att = jnp.concatenate([units[index] for index in range(CTX)], axis=1)
    pack_ref[CTX + 1] = att
    pack_ref[CTX + 3] = dy_ref[...]
    pack_ref[CTX + 4] = h_one_ref[...]
    wait_all(copies[0])
    for chunk in range(CTX):
        held_out[:, chunk * GROUP : (chunk + 1) * GROUP] = out_parts[chunk, :, :GROUP]
    mid = x_ref[...].astype(WIDE) + mm(att, held_out[...]) + vec[6:7]
    centred, inverse = moments(mid)
    normed = centred * inverse
    pack_ref[CTX] = (normed * vec[2:3] + vec[3:4]).astype(LOW)
    total[...] = mid + vec[7:8]
    back[...] = jnp.zeros_like(back)
    for group in copies[1:]:
        wait_all(group)
    side = FF_SIDE

    def chunk_step(chunk, carry):
        pre = mm(pack_ref[CTX], held_fc[chunk]) + bias[chunk]
        square = pre * pre
        tanh = jnp.tanh(0.7978845608028654 * (pre + 0.044715 * square * pre))
        act = (0.5 * pre * (1.0 + tanh)).astype(LOW)
        slope = 0.5 * (1.0 + tanh) + 0.5 * pre * (1.0 - tanh * tanh) * (
            0.7978845608028654 * (1.0 + 3.0 * 0.044715 * square)
        )
        grads = []
        for half in range(2):
            weight = held_proj[2 * chunk + half]
            part = act[:, half * side : (half + 1) * side]
            acts[2 * chunk + half] = part
            total[...] += mt(part, weight)
            grads.append(mm(dy_ref[...], weight))
        dpre = (jnp.concatenate(grads, axis=1) * slope).astype(LOW)
        pack_ref[chunk] = dpre
        dbias_ref[chunk] = jnp.sum(dpre.astype(WIDE), axis=0, keepdims=True)
        back[...] += mt(dpre, held_fc[chunk])
        return carry

    lax.fori_loop(0, CTX, chunk_step, 0)
    out_ref[...] = total[...].astype(LOW)
    core = meta[0] & 1
    for chunk in range(CTX):
        mine[chunk] = acts[2 * chunk + core]
        theirs[chunk] = acts[2 * chunk + 1 - core]
    grad = back[...]
    dy = dy_ref[...].astype(WIDE)
    dmid = dy + norm_back(grad, normed, inverse, vec[2:3])
    dmid_ref[...] = dmid
    datt = dmid.astype(LOW)
    pack_ref[CTX + 2] = datt
    rows_ref[0:1] = jnp.sum(grad * normed, axis=0, keepdims=True)
    rows_ref[1:2] = jnp.sum(grad, axis=0, keepdims=True)
    rows_ref[2:3] = jnp.sum(datt.astype(WIDE), axis=0, keepdims=True)
    rows_ref[3:4] = jnp.sum(dy, axis=0, keepdims=True)
    rows_ref[4:8] = jnp.zeros((4, WIDTH), WIDE)
    dout = mt(datt, held_out[...]).astype(LOW)
    for index in range(CTX):
        units[index] = dout[:, index * GROUP : (index + 1) * GROUP]
    for ctx, target in enumerate(results):
        write_packed(target, units[meta[1] ^ ctx])


def mlp_grad_kernel(meta, *refs):
    acts, packs, targets = refs[:2], refs[2:4], refs[4:8]
    held_out, held_fc, held_proj, turn, sems = refs[8:]
    dy = [turned(pack[CTX + 3]) for pack in packs]
    for chunk in range(CTX):
        held_proj[chunk] = over_both(dy, [act[chunk] for act in acts]).astype(LOW)
    left = half_rows(meta, [pack[CTX] for pack in packs], turn)
    for chunk in range(CTX):
        held_fc[chunk] = over_both(left, [pack[chunk] for pack in packs]).astype(LOW)
    left = half_rows(meta, [pack[CTX + 1] for pack in packs], turn)
    grad = over_both(left, [pack[CTX + 2] for pack in packs]).astype(LOW)
    for chunk in range(CTX):
        held_out[chunk, :, :GROUP] = grad[:, chunk * GROUP : (chunk + 1) * GROUP]
        held_out[chunk, :, GROUP:] = jnp.zeros((WIDTH // 2, TILE - GROUP), LOW)

    def place(part, ctx):
        ctx = meta[1] ^ ctx
        chunk = (meta[0] ^ (2 * part)) // 2
        rows = pl.ds(part * ROWS, ROWS)
        return [
            (pl.ds(WIDTH + 2 * FF_SIDE, TILE), held_out.at[ctx, rows, :]),
            (pl.ds(0, WIDTH), held_fc.at[ctx, rows, :]),
            (pl.ds(WIDTH, FF_SIDE), held_proj.at[chunk, rows_of(2 * ctx, ROWS), :]),
            (pl.ds(WIDTH + FF_SIDE, FF_SIDE), held_proj.at[chunk, rows_of(2 * ctx + 1, ROWS), :]),
        ]

    store_grad(place, targets, sems)


def qkv_grad_kernel(meta, *refs):
    pack, own, came, targets = refs[:2], refs[2:4], refs[4:6], refs[6:10]
    mixed_ref, dbias_ref, held, units, turn, sems = refs[10:]
    for core in range(2):
        for ctx in range(CTX):
            value = read_packed(own[core] if ctx == 0 else came[core].at[ctx - 1])
            for part in range(3):
                units[core, CTX * part + (meta[1] ^ ctx)] = value[
                    :, part * GROUP : (part + 1) * GROUP
                ]
    left = half_rows(meta, [pack[0][...], pack[1][...]], turn)
    for chunk in range(CTX):
        mixed = [
            jnp.concatenate([units[core, 3 * chunk + part] for part in range(3)], axis=1)
            for core in range(2)
        ]
        mixed_ref[chunk] = mixed[0]
        bias = jnp.sum(mixed[0].astype(WIDE), axis=0, keepdims=True)
        for part in range(3):
            dbias_ref[3 * chunk + part] = bias[:, part * GROUP : (part + 1) * GROUP]
        held[chunk] = over_both(left, mixed).astype(LOW)

    def place(part, ctx):
        return [(pl.ds(0, 3 * GROUP), held.at[meta[1] ^ ctx, pl.ds(part * ROWS, ROWS), :])]

    store_grad(place, targets, sems)


def input_grad_kernel(meta, x_ref, dmid_ref, mixed_ref, rows_ref, dfc_ref, dqkv_ref, *refs):
    vectors, parts, refs = refs[:4], refs[4 : 4 + PARTS], refs[4 + PARTS :]
    grad_ref, results, (held, chunks, rows, sums, sems) = refs[0], refs[1:5], refs[5:]
    (copies,) = load_weight(meta, parts, functools.partial(qkv_place, held), sems, meta[1])
    params = read_vectors(meta, vectors, chunks)
    centred, inverse = moments(x_ref[...].astype(WIDE))
    normed = centred * inverse
    wait_all(copies)
    grad = jnp.zeros((TOKENS, WIDTH), WIDE)
    for chunk in range(CTX):
        grad = grad + mt(mixed_ref[chunk], held[chunk])
    grad_ref[...] = dmid_ref[...] + norm_back(grad, normed, inverse, params[0:1])
    rows[0:1] = jnp.sum(grad * normed, axis=0, keepdims=True)
    rows[1:2] = jnp.sum(grad, axis=0, keepdims=True)
    rows[2:4] = rows_ref[0:2]
    for chunk in range(CTX):
        lanes = slice(chunk * GROUP, (chunk + 1) * GROUP)
        rows[4:5, lanes] = dqkv_ref[chunk]
        rows[5:6, lanes] = dqkv_ref[2 * CTX + chunk]
        rows[8 + chunk : 9 + chunk] = dfc_ref[chunk]
    rows[6:8] = rows_ref[2:4]
    rows[12:16] = jnp.zeros((4, WIDTH), WIDE)
    for chunk in range(CTX):
        sums[chunk] = rows[:, chunk * GROUP : (chunk + 1) * GROUP]
    for ctx, target in enumerate(results):
        target[...] = sums[meta[1] ^ ctx]


def sum_kernel(one_kept, one_back, two_kept, two_back, one_keep, one_send, two_keep, two_send):
    pairs = ((one_kept, one_back, one_keep, one_send), (two_kept, two_back, two_keep, two_send))
    for kept, back, keep, send in pairs:
        keep[...] = kept[0].astype(WIDE) + back[0].astype(WIDE)
        send[...] = (kept[1].astype(WIDE) + back[1].astype(WIDE)).astype(LOW)


def shape_of(dtype, *dims):
    return jax.ShapeDtypeStruct(dims, dtype)


def call(kernel, arguments, kinds, outputs, out_kinds, scratch):
    spec = {
        "v": pl.BlockSpec(memory_space=pltpu.VMEM),
        "s": pl.BlockSpec(memory_space=pltpu.SMEM),
        "a": pl.BlockSpec(memory_space=pl.ANY),
        "h": pl.BlockSpec((None, TOKENS, WIDTH), lambda step: (CTX + 4, 0, 0)),
    }
    return pl.pallas_call(
        kernel,
        grid=(1,),
        out_shape=tuple(outputs),
        in_specs=[spec[kind] for kind in kinds],
        out_specs=tuple(spec[kind] for kind in out_kinds),
        scratch_shapes=scratch,
        cost_estimate=pl.CostEstimate(flops=1, bytes_accessed=1, transcendentals=0),
        compiler_params=pltpu.CompilerParams(vmem_limit_bytes=VMEM_LIMIT),
    )(*arguments)


def local_fast(
    block_in,
    cotangent,
    w_qkv,
    w_out,
    w_fc,
    w_proj,
    vectors,
    qkv_first,
    qkv_second,
    out_first,
    out_second,
    fc_first,
    fc_second,
    proj_first,
    proj_second,
    vec_first,
    vec_second,
):
    batch, ctx = lax.axis_index("batch"), lax.axis_index("ctx")
    meta = jnp.stack([batch, ctx]).astype(jnp.int32)
    inputs = block_in.reshape(TOKENS, WIDTH)
    grad_low = cotangent.reshape(TOKENS, WIDTH)
    tie = lax.optimization_barrier

    qkv_sems = pltpu.SemaphoreType.DMA((1, BATCH * CTX))
    mlp_sems = pltpu.SemaphoreType.DMA((4, BATCH * CTX))
    qkv_held = pltpu.VMEM((CTX, WIDTH, 3 * GROUP), LOW)
    vec_held = pltpu.VMEM((CTX, 16, GROUP), WIDE)

    low_vec = jnp.pad(vectors.astype(LOW), ((0, 4), (0, 0)))
    low_vec = [low_vec[:, start : start + HEAD] for start in range(0, GROUP, HEAD)]
    low_vec = jnp.concatenate(low_vec + [jnp.zeros((ROWS - 48, HEAD), LOW)], axis=0)
    piece_one = jnp.concatenate([w_qkv.astype(LOW), low_vec], axis=1)
    low_proj = w_proj.astype(LOW).T
    piece_two = jnp.concatenate(
        [
            w_fc.astype(LOW),
            low_proj[:ROWS],
            low_proj[ROWS:],
            w_out.astype(LOW),
            jnp.zeros((ROWS, TILE - GROUP), LOW),
        ],
        axis=1,
    )
    parts_one = (piece_one,) + exchange(piece_one)
    vec_parts = [part[:48, 3 * GROUP :] for part in parts_one]
    own_one = jnp.stack([part[:, : 3 * GROUP] for part in parts_one])
    piece_two, late_vec = tie((piece_two, vec_parts))
    own_two = lax.all_gather(piece_two, "ctx", axis=0)
    x_one, y_one = gather_first(own_one)
    parts_one = [own_one, x_one, y_one, *gather_second(x_one, y_one)]
    parts_one = parts_one + to_core(parts_one)

    packed = shape_of(LOW, TOKENS * 3 * GROUP // LANES, LANES)
    single = shape_of(LOW, TOKENS * GROUP // LANES, LANES)
    tokens_low = shape_of(LOW, TOKENS, WIDTH)
    hidden_low = shape_of(LOW, CTX, TOKENS, WIDTH)
    h_one, own, *sent = call(
        qkv_kernel,
        (meta, inputs, *vec_parts, *parts_one),
        "s" + "v" * 5 + "a" * PARTS,
        [tokens_low] + [packed] * 4,
        "v" * 5,
        [qkv_held, pltpu.VMEM((CTX, TOKENS, 3 * GROUP), LOW), vec_held, qkv_sems],
    )
    qkv_pieces = [own] + [swap(part, "ctx", bit) for bit, part in zip((1, 2, 3), sent)]

    own_two, late_h = tie((own_two, h_one))
    x_two, y_two = gather_first(own_two)
    qkv_pieces, x_two, y_two = tie((qkv_pieces, x_two, y_two))
    across_two = gather_second(x_two, y_two)
    parts_two = [own_two, x_two, y_two]
    swapped_two = to_core(parts_two)

    sequence_low = pltpu.VMEM((SPAN, GROUP), LOW)
    sequence_wide = pltpu.VMEM((SPAN, GROUP), WIDE)
    own, *sent = call(
        attend_kernel,
        (meta, *qkv_pieces),
        "s" + "v" * 4,
        [single] * 4,
        "v" * 4,
        [sequence_low] * 3 + [sequence_wide],
    )
    sent, swapped_two = tie((sent, swapped_two))
    att_pieces = [own] + [swap(part, "ctx", bit) for bit, part in zip((1, 2, 3), sent)]
    across_two, att_pieces = tie((across_two, att_pieces))
    parts_two = parts_two + list(across_two) + swapped_two + to_core(across_two)

    pack_shape = shape_of(LOW, CTX + 5, TOKENS, WIDTH)
    act_shape = shape_of(LOW, BATCH // 2, TOKENS, FF_SIDE)
    out, pack, act_mine, act_theirs, dmid, own, *sent = call(
        middle_kernel,
        (meta, inputs, grad_low, late_h, *vec_parts, *att_pieces, *parts_two),
        "s" + "v" * 11 + "a" * PARTS,
        [tokens_low, pack_shape, act_shape, act_shape, shape_of(WIDE, TOKENS, WIDTH)]
        + [single] * 4
        + [shape_of(WIDE, 8, WIDTH), shape_of(WIDE, CTX, 1, WIDTH)],
        "v" * 11,
        [
            pltpu.VMEM((CTX, WIDTH, TILE), LOW),
            pltpu.VMEM((WIDTH, WIDTH), LOW),
            pltpu.VMEM((CTX, WIDTH, WIDTH), LOW),
            pltpu.VMEM((BATCH, WIDTH, FF_SIDE), LOW),
            pltpu.VMEM((CTX, TOKENS, GROUP), LOW),
            pltpu.VMEM((TOKENS, WIDTH), WIDE),
            pltpu.VMEM((TOKENS, WIDTH), WIDE),
            vec_held,
            pltpu.VMEM((CTX, 1, WIDTH), WIDE),
            pltpu.VMEM((BATCH, TOKENS, FF_SIDE), LOW),
            mlp_sems,
        ],
    )
    sent, (rows_two, dbias_fc) = sent[:3], sent[3:]
    grad_pieces = [own] + [swap(part, "ctx", bit) for bit, part in zip((1, 2, 3), sent)]
    act_came, pack_came = swap(act_theirs, "batch", CORE), swap(pack, "batch", CORE)

    half_sems = BATCH * CTX // 2
    turn_held = pltpu.VMEM((2, WIDTH, TOKENS), LOW)
    mlp_parts = call(
        mlp_grad_kernel,
        (meta, act_mine, act_came, pack, pack_came),
        "s" + "v" * 4,
        [shape_of(LOW, 2, 2, ROWS, MLP)] * 4,
        "aaaa",
        [
            pltpu.VMEM((CTX, WIDTH // 2, TILE), LOW),
            pltpu.VMEM((CTX, WIDTH // 2, WIDTH), LOW),
            pltpu.VMEM((BATCH // 2, WIDTH, FF_SIDE), LOW),
            turn_held,
            pltpu.SemaphoreType.DMA((4, half_sems)),
        ],
    )
    mlp_parts, grad_pieces = tie((mlp_parts, grad_pieces))
    mlp_kept = mlp_parts[0], mlp_parts[2]
    mlp_back = swap_pair((mlp_parts[1], mlp_parts[3]), YBIT, XBIT)
    own, *sent = call(
        attend_back_kernel,
        (meta, *qkv_pieces, *grad_pieces),
        "s" + "v" * 8,
        [packed] * 4,
        "v" * 4,
        [sequence_low] * 4 + [sequence_wide] * 3,
    )
    own_came = swap(own, "batch", CORE)
    received = [swap(part, "ctx", bit) for bit, part in zip((1, 2, 3), sent)]
    mlp_back, received[0] = tie((mlp_back, received[0]))
    pair = [shape_of(WIDE, 2, ROWS, MLP), shape_of(LOW, 2, ROWS, MLP)]
    one_keep, one_send, two_keep, two_send = call(
        sum_kernel,
        (mlp_kept[0], mlp_back[0], mlp_kept[1], mlp_back[1]),
        "vvvv",
        pair + pair,
        "vvvv",
        [],
    )
    one_keep, received[1], received[2] = tie((one_keep, received[1], received[2]))
    mlp_back = swap_pair((one_send, two_send), XBIT, YBIT)
    received = jnp.stack(received)
    received_came = swap(received, "batch", CORE)

    *qkv_parts, mixed, dbias_qkv = call(
        qkv_grad_kernel,
        (meta, pack, pack_came, own, own_came, received, received_came),
        "shhvvvv",
        [shape_of(LOW, 2, 2, ROWS, 3 * GROUP)] * 4
        + [shape_of(LOW, CTX, TOKENS, 3 * GROUP), shape_of(WIDE, 3 * CTX, 1, GROUP)],
        "aaaavv",
        [
            pltpu.VMEM((CTX, WIDTH // 2, 3 * GROUP), LOW),
            pltpu.VMEM((2, 3 * CTX, TOKENS, GROUP), LOW),
            turn_held,
            pltpu.SemaphoreType.DMA((1, half_sems)),
        ],
    )
    qkv_kept = qkv_parts[0], qkv_parts[2]
    mlp_back, qkv_parts = tie((mlp_back, qkv_parts))
    mlp_one, mlp_two = scatter_near((one_keep, two_keep), mlp_back)
    qkv_kept = qkv_parts[0], qkv_parts[2]
    qkv_back = swap_pair((qkv_parts[1], qkv_parts[3]), YBIT, XBIT)
    grad_input, own, *sent = call(
        input_grad_kernel,
        (meta, inputs, dmid, mixed, rows_two, dbias_fc, dbias_qkv, *late_vec, *parts_one),
        "s" + "v" * 10 + "a" * PARTS,
        [shape_of(WIDE, TOKENS, WIDTH)] + [shape_of(WIDE, 16, GROUP)] * 4,
        "v" * 5,
        [qkv_held, vec_held, pltpu.VMEM((16, WIDTH), WIDE), vec_held, qkv_sems],
    )
    qkv_kept, qkv_sent = scatter_second(qkv_kept, qkv_back)
    qkv_back = swap_pair(qkv_sent, XBIT, YBIT)
    qkv_back, own, sent = tie((qkv_back, own, sent))
    mlp_grad = scatter_far(mlp_one, mlp_two)
    qkv_grad = scatter_far(*scatter_near(qkv_kept, qkv_back))

    vec_grad = own + sum(swap(part, "ctx", bit) for bit, part in zip((1, 2, 3), sent))
    for bit in (CORE, XBIT, YBIT):
        vec_grad = vec_grad + swap(vec_grad, "batch", bit)
    vec_grad = vec_grad[:12]
    fc_grad = mlp_grad[:, :WIDTH]
    proj_grad = jnp.concatenate(
        [mlp_grad[:, WIDTH : WIDTH + FF_SIDE], mlp_grad[:, WIDTH + FF_SIDE : WIDTH + 2 * FF_SIDE]],
        axis=0,
    )
    out_grad = mlp_grad[:, WIDTH + 2 * FF_SIDE : WIDTH + 2 * FF_SIDE + GROUP]

    qkv_m, qkv_s, qkv_w = adamw(w_qkv, qkv_grad, qkv_first, qkv_second, 0.06, 0.1)
    out_m, out_s, out_w = adamw(w_out, out_grad, out_first, out_second, 0.06, 0.1)
    fc_m, fc_s, fc_w = adamw(w_fc, fc_grad, fc_first, fc_second, 0.06, 0.1)
    proj_m, proj_s, proj_w = adamw(w_proj, proj_grad.T, proj_first, proj_second, 0.06, 0.1)
    vec_m, vec_s, vec_w = adamw(vectors, vec_grad, vec_first, vec_second, 0.2, 0.0)
    return (
        out.reshape(block_in.shape),
        grad_input.reshape(block_in.shape),
        qkv_m,
        qkv_s,
        qkv_w,
        out_m,
        out_s,
        out_w,
        fc_m,
        fc_s,
        fc_w,
        proj_m,
        proj_s,
        proj_w,
        vec_m,
        vec_s,
        vec_w,
    )


def solution(mesh):
    in_specs = (
        P("batch", "ctx", None, None),
        P("batch", "ctx", None, None),
        P("batch", "ctx"),
        P("batch", "ctx"),
        P("batch", "ctx"),
        P("batch", "ctx"),
        P(None, "ctx"),
        P("batch", "ctx"),
        P("batch", "ctx"),
        P("batch", "ctx"),
        P("batch", "ctx"),
        P("batch", "ctx"),
        P("batch", "ctx"),
        P("batch", "ctx"),
        P("batch", "ctx"),
        P(None, "ctx"),
        P(None, "ctx"),
    )
    out_specs = (
        P("batch", "ctx", None, None),
        P("batch", "ctx", None, None),
        P("batch", "ctx"),
        P("batch", "ctx"),
        P("batch", "ctx"),
        P("batch", "ctx"),
        P("batch", "ctx"),
        P("batch", "ctx"),
        P("batch", "ctx"),
        P("batch", "ctx"),
        P("batch", "ctx"),
        P("batch", "ctx"),
        P("batch", "ctx"),
        P("batch", "ctx"),
        P(None, "ctx"),
        P(None, "ctx"),
        P(None, "ctx"),
    )
    sizes = (mesh.shape["batch"], mesh.shape["ctx"])
    local = local_fast if sizes == (BATCH, CTX) else local_any
    return jax.shard_map(local, mesh=mesh, in_specs=in_specs, out_specs=out_specs, check_vma=False)
```

profile of v0, /device:TPU:0, one launch (start us, length us, event | category | flops | bytes accessed | tf_op | source)
XLA Modules:
  0.0 301.4 jit_solution(14049648601684024763)
XLA Ops:
  9.2 5.1 %collective-permute-start.2 = (bf16[96,640]{1,0:T(8,128)(2,1)S(1)}, bf16[96,640]{1,0:T(8,128)(2,1)S(1)}, u32[]{:S(2)}, u32[]{:S(2)}) collective-permute-start(bf16[96,640]{1,0:T(8,128)(2,1)S(1)} %maximum_maximum_fusion), channel_id=1, source_target_pairs={{0,3},{1,2},{2,1},{3,0},{4,7},{5,6},{6,5},{7,4},{8,11},{9,10},{10,... | collective-permute-start | bytes 368648 | tf_op jit(solution)/shard_map/ppermute | solution.py:341
  17.4 1.1 collective-permute-done.2
  19.2 5.4 %collective-permute-done.1 = bf16[96,640]{1,0:T(8,128)(2,1)S(1)} collective-permute-done((bf16[96,640]{1,0:T(8,128)(2,1)S(1)}, bf16[96,640]{1,0:T(8,128)(2,1)S(1)}, u32[]{:S(2)}, u32[]{:S(2)}) %collective-permute-start.1) | collective-permute-done | bytes 122912 | tf_op jit(solution)/shard_map/ppermute | solution.py:341
  26.2 1.6 collective-permute-start.4
  27.8 1.5 collective-permute-start.3
  29.3 9.3 %collective-permute-done.4.refs_6_ = bf16[4,96,576]{2,1,0:T(8,128)(2,1)S(1)} collective-permute-done((bf16[4,96,576]{2,1,0:T(8,128)(2,1)S(1)}, bf16[4,96,576]{2,1,0:T(8,128)(2,1)S(1)}, u32[]{:S(2)}, u32[]{:S(2)}) %collective-permute-start.4) | collective-permute-done | bytes 442400 | tf_op jit(solution)/shard_map/ppermute | solution.py:341
  38.6 1.6 collective-permute-start.6
  40.2 1.6 collective-permute-start.5
  42.0 3.2 %collective-permute-done.6.refs_8_ = bf16[2,96,576]{2,1,0:T(8,128)(2,1)} collective-permute-done((bf16[2,96,576]{2,1,0:T(8,128)(2,1)S(1)}, bf16[2,96,576]{2,1,0:T(8,128)(2,1)}, u32[]{:S(2)}, u32[]{:S(2)}) %collective-permute-start.6) | collective-permute-done | bytes 221216 | tf_op jit(solution)/shard_map/ppermute | solution.py:341
  45.2 3.5 %collective-permute-done.5.refs_7_ = bf16[2,96,576]{2,1,0:T(8,128)(2,1)} collective-permute-done((bf16[2,96,576]{2,1,0:T(8,128)(2,1)S(1)}, bf16[2,96,576]{2,1,0:T(8,128)(2,1)}, u32[]{:S(2)}, u32[]{:S(2)}) %collective-permute-start.5) | collective-permute-done | bytes 221216 | tf_op jit(solution)/shard_map/ppermute | solution.py:341
  49.4 1.2 collective-permute-done.10.refs_12_
  51.4 6.2 %shard_map.296 = (bf16[256,768]{1,0:T(8,128)(2,1)}, bf16[1152,128]{1,0:T(8,128)(2,1)}, bf16[1152,128]{1,0:T(8,128)(2,1)}, bf16[1152,128]{1,0:T(8,128)(2,1)}, bf16[1152,128]{1,0:T(8,128)(2,1)}) custom-call(s32[2]{0:T(128)} %pad_add_fusion.meta, bf16[256,768]{1,0:T(8,128)(2,1)} %bitcast.62, bf16[48,64]{1,0:T(8,128)(2,1)} %pad_maximum_fusion.2.refs_0_, ...), custom_call_target="tpu_custom_call" | custom-call | flops 1 | bytes 1 | tf_op jit(solution)/shard_map/pallas_call | solution.py:813
  57.6 2.5 all-gather.3.cloned.1.call-done
  60.1 1.5 collective-permute-start.16
  61.6 1.5 collective-permute-start.15
  63.7 1.2 collective-permute-start.13
  65.0 2.5 collective-permute-start.14
  67.5 8.4 %collective-permute-done.12.refs_1_ = bf16[1152,128]{1,0:T(8,128)(2,1)S(1)} collective-permute-done((bf16[1152,128]{1,0:T(8,128)(2,1)}, bf16[1152,128]{1,0:T(8,128)(2,1)S(1)}, u32[]{:S(2)}, u32[]{:S(2)}) %collective-permute-start.12) | collective-permute-done | bytes 294944 | tf_op jit(solution)/shard_map/ppermute | solution.py:341
  75.9 11.6 %collective-permute-done.13.refs_2_ = bf16[1152,128]{1,0:T(8,128)(2,1)S(1)} collective-permute-done((bf16[1152,128]{1,0:T(8,128)(2,1)}, bf16[1152,128]{1,0:T(8,128)(2,1)S(1)}, u32[]{:S(2)}, u32[]{:S(2)}) %collective-permute-start.13) | collective-permute-done | bytes 294944 | tf_op jit(solution)/shard_map/ppermute | solution.py:341
  87.4 4.1 %collective-permute-done.16.refs_10_ = bf16[4,96,1792]{2,1,0:T(8,128)(2,1)S(1)} collective-permute-done((bf16[4,96,1792]{2,1,0:T(8,128)(2,1)}, bf16[4,96,1792]{2,1,0:T(8,128)(2,1)S(1)}, u32[]{:S(2)}, u32[]{:S(2)}) %collective-permute-start.16) | collective-permute-done | bytes 1376288 | tf_op jit(solution)/shard_map/ppermute | solution.py:341
  91.6 1.2 collective-permute-done.15.refs_9_
  95.1 1.5 collective-permute-start.18
  97.2 6.1 %shard_map.297 = (bf16[384,128]{1,0:T(8,128)(2,1)}, bf16[384,128]{1,0:T(8,128)(2,1)}, bf16[384,128]{1,0:T(8,128)(2,1)}, bf16[384,128]{1,0:T(8,128)(2,1)}) custom-call(s32[2]{0:T(128)} %pad_add_fusion.meta, bf16[1152,128]{1,0:T(8,128)(2,1)} %get-tuple-element.121.refs_0_, bf16[1152,128]{1,0:T(8,128)(2,1)} %copy-done.20, bf16[1152,128]{1,0:T(8,128)(2,1)} %copy-done.21, ...), custom_call_target="tpu_custom_call" | custom-call | flops 1 | bytes 1 | tf_op jit(solution)/shard_map/pallas_call | solution.py:813
  103.3 1.2 collective-permute-start.22
  104.5 1.6 collective-permute-start.23
  106.2 1.6 collective-permute-start.24
  107.8 5.0 %collective-permute-done.18.refs_12_ = bf16[2,96,1792]{2,1,0:T(8,128)(2,1)} collective-permute-done((bf16[2,96,1792]{2,1,0:T(8,128)(2,1)}, bf16[2,96,1792]{2,1,0:T(8,128)(2,1)}, u32[]{:S(2)}, u32[]{:S(2)}) %collective-permute-start.18) | collective-permute-done | bytes 688160 | tf_op jit(solution)/shard_map/ppermute | solution.py:341
  112.8 1.2 collective-permute-done.17.refs_11_
  115.4 1.8 collective-permute-done.25.refs_16_
  119.0 18.0 %shard_map.298 = (bf16[256,768]{1,0:T(8,128)(2,1)}, bf16[9,256,768]{2,1,0:T(8,128)(2,1)}, bf16[4,256,384]{2,1,0:T(8,128)(2,1)}, bf16[4,256,384]{2,1,0:T(8,128)(2...) custom-call(s32[2]{0:T(128)} %pad_add_fusion.meta, ...), custom_call_target="tpu_custom_call" | custom-call | flops 1 | bytes 1 | tf_op jit(solution)/shard_map/pallas_call | solution.py:813
  137.6 1.6 collective-permute-start.29
  139.2 1.3 collective-permute-start.30
  140.4 1.6 collective-permute-start.31
  142.0 2.7 collective-permute-done.28.refs_1_
  145.5 1.2 copy-done
  146.7 10.0 %shard_map.299 = (bf16[2,2,96,1792]{3,2,1,0:T(8,128)(2,1)}, bf16[2,2,96,1792]{3,2,1,0:T(8,128)(2,1)}, bf16[2,2,96,1792]{3,2,1,0:T(8,128)(2,1)}, bf16[2,2,96,1792]{3,2,1,0:T(8,128)(2,1)}) custom-call(s32[2]{0:T(128)} %pad_add_fusion.meta, bf16[4,256,384]{2,1,0:T(8,128)(2,1)} %get-tuple-element.144.refs_0_, bf16[4,256,384]{2,1,0:T(8,128)(2,1)} %copy-done.24, ...), custom_call_target="tpu_custom_call" | custom-call | flops 1 | bytes 1 | tf_op jit(solution)/shard_map/pallas_call | solution.py:813
  156.8 1.5 collective-permute-start.33
  158.9 21.8 %shard_map.300 = (bf16[1152,128]{1,0:T(8,128)(2,1)}, bf16[1152,128]{1,0:T(8,128)(2,1)}, bf16[1152,128]{1,0:T(8,128)(2,1)}, bf16[1152,128]{1,0:T(8,128)(2,1)}) custom-call(s32[2]{0:T(128)} %pad_add_fusion.meta, bf16[1152,128]{1,0:T(8,128)(2,1)} %get-tuple-element.121.refs_0_, bf16[1152,128]{1,0:T(8,128)(2,1)} %copy-done.20, bf16[1152,128]{1,0:T(8,128)(2,1)} %copy-done.21, ...), custom_call_target="tpu_custom_call" | custom-call | flops 1 | bytes 1 | tf_op jit(solution)/shard_map/pallas_call | solution.py:813
  180.6 1.6 collective-permute-start.35
  182.2 1.3 collective-permute-start.36
  183.5 1.6 collective-permute-start.37
  185.0 9.7 %collective-permute-done.35 = bf16[1152,128]{1,0:T(8,128)(2,1)S(1)} collective-permute-done((bf16[1152,128]{1,0:T(8,128)(2,1)}, bf16[1152,128]{1,0:T(8,128)(2,1)S(1)}, u32[]{:S(2)}, u32[]{:S(2)}) %collective-permute-start.35) | collective-permute-done | bytes 294944 | tf_op jit(solution)/shard_map/ppermute | solution.py:341
  194.7 1.1 copy-done.16
  195.8 1.1 copy-done.17
  196.9 4.8 %shard_map.301 = (f32[2,96,1792]{2,1,0:T(8,128)}, bf16[2,96,1792]{2,1,0:T(8,128)(2,1)}, f32[2,96,1792]{2,1,0:T(8,128)}, bf16[2,96,1792]{2,1,0:T(8,128)(2,1)}) custom-call(bf16[2,2,96,1792]{3,2,1,0:T(8,128)(2,1)} %get-tuple-element.163.one_kept, bf16[2,2,96,1792]{3,2,1,0:T(8,128)(2,1)} %copy-done.16, bf16[2,2,96,1792]{3,2,1,0:T(8,128)(2,1)} %get-tuple-element.165.two_kept, ...), custom_call_target="tpu_custom_call" | custom-call | flops 1 | bytes 1 | tf_op jit(solution)/shard_map/pallas_call | solution.py:813
  201.7 4.2 %collective-permute-done.36 = bf16[1152,128]{1,0:T(8,128)(2,1)S(1)} collective-permute-done((bf16[1152,128]{1,0:T(8,128)(2,1)}, bf16[1152,128]{1,0:T(8,128)(2,1)S(1)}, u32[]{:S(2)}, u32[]{:S(2)}) %collective-permute-start.36) | collective-permute-done | bytes 294944 | tf_op jit(solution)/shard_map/ppermute | solution.py:341
  206.1 1.5 collective-permute-start.39
  208.2 1.6 collective-permute-done.32.refs_3_
  211.4 6.5 %shard_map.302 = (bf16[2,2,96,576]{3,2,1,0:T(8,128)(2,1)}, bf16[2,2,96,576]{3,2,1,0:T(8,128)(2,1)}, bf16[2,2,96,576]{3,2,1,0:T(8,128)(2,1)}, bf16[2,2,96,576]{3,...) custom-call(s32[2]{0:T(128)} %pad_add_fusion.meta, ...), custom_call_target="tpu_custom_call" | custom-call | flops 1 | bytes 1 | tf_op jit(solution)/shard_map/pallas_call | solution.py:813
  217.9 6.0 %collective-permute-done.39 = bf16[2,96,1792]{2,1,0:T(8,128)(2,1)S(1)} collective-permute-done((bf16[2,96,1792]{2,1,0:T(8,128)(2,1)S(1)}, bf16[2,96,1792]{2,1,0:T(8,128)(2,1)S(1)}, u32[]{:S(2)}, u32[]{:S(2)}) %collective-permute-start.39) | collective-permute-done | bytes 688160 | tf_op jit(solution)/shard_map/ppermute | solution.py:341
  223.9 1.2 collective-permute-done.40
  226.2 11.6 %collective-permute-done.41 = bf16[2,2,96,576]{3,2,1,0:T(8,128)(2,1)S(1)} collective-permute-done((bf16[2,2,96,576]{3,2,1,0:T(8,128)(2,1)}, bf16[2,2,96,576]{3,2,1,0:T(8,128)(2,1)S(1)}, u32[]{:S(2)}, u32[]{:S(2)}) %collective-permute-start.41) | collective-permute-done | bytes 442400 | tf_op jit(solution)/shard_map/ppermute | solution.py:341
  237.8 1.1 convert_add_fusion.2
  240.5 5.3 %collective-permute-start.47 = (bf16[2,96,1792]{2,1,0:T(8,128)(2,1)S(1)}, bf16[2,96,1792]{2,1,0:T(8,128)(2,1)S(1)}, u32[]{:S(2)}, u32[]{:S(2)}) collective-permute-start(bf16[2,96,1792]{2,1,0:T(8,128)(2,1)S(1)} %add_convert_fusion), channel_id=1, source_target_pairs={{0,1},{1,0},{2,3},{3,2},{4,5},{5,4},{6,7},{7,6},{8,9},{9,8},{10,11... | collective-permute-start | bytes 2064392 | tf_op jit(solution)/shard_map/ppermute | solution.py:341
  245.8 7.0 %shard_map.303 = (f32[256,768]{1,0:T(8,128)}, f32[16,192]{1,0:T(8,128)}, f32[16,192]{1,0:T(8,128)}, f32[16,192]{1,0:T(8,128)}, f32[16,192]{1,0:T(8,128)}) custom-call(s32[2]{0:T(128)} %pad_add_fusion.meta, bf16[256,768]{1,0:T(8,128)(2,1)} %bitcast.64, f32[256,768]{1,0:T(8,128)} %get-tuple-element.142.dmid_ref, ...), custom_call_target="tpu_custom_call" | custom-call | flops 1 | bytes 1 | tf_op jit(solution)/shard_map/pallas_call | solution.py:813
  252.9 2.9 collective-permute-start.50
  255.8 1.5 collective-permute-start.51
  257.2 3.3 %collective-permute-done.49 = f32[16,192]{1,0:T(8,128)S(1)} collective-permute-done((f32[16,192]{1,0:T(8,128)}, f32[16,192]{1,0:T(8,128)S(1)}, u32[]{:S(2)}, u32[]{:S(2)}) %collective-permute-start.49) | collective-permute-done | bytes 12320 | tf_op jit(solution)/shard_map/ppermute | solution.py:341
  260.5 2.3 collective-permute-done.51
  266.0 1.1 collective-permute-start.48
  267.1 1.3 collective-permute-done.53
  268.4 1.1 collective-permute-start.54
  269.5 4.9 %collective-permute-done.45 = bf16[2,96,576]{2,1,0:T(8,128)(2,1)S(1)} collective-permute-done((bf16[2,96,576]{2,1,0:T(8,128)(2,1)S(1)}, bf16[2,96,576]{2,1,0:T(8,128)(2,1)S(1)}, u32[]{:S(2)}, u32[]{:S(2)}) %collective-permute-start.45) | collective-permute-done | bytes 221216 | tf_op jit(solution)/shard_map/ppermute | solution.py:341
  275.7 13.8 %collective-permute-done.46 = bf16[96,576]{1,0:T(8,128)(2,1)S(1)} collective-permute-done((bf16[96,576]{1,0:T(8,128)(2,1)S(1)}, bf16[96,576]{1,0:T(8,128)(2,1)S(1)}, u32[]{:S(2)}, u32[]{:S(2)}) %collective-permute-start.46) | collective-permute-done | bytes 110624 | tf_op jit(solution)/shard_map/ppermute | solution.py:341
  (205 shorter events, 32.1 us)
Async XLA Ops:
  7.2 52.9 %all-gather.3.cloned.1.call-start = ((), (), s32[]{:S(2)}) async-start(), calls=%async_computation | async-start | bytes 1720320 | tf_op jit(solution)/shard_map/all_gather | solution.py:874
  9.1 16.9 %copy-start.7 = (f32[96,576]{1,0:T(8,128)S(1)}, f32[96,576]{1,0:T(8,128)}, u32[]{:S(2)}) copy-start(f32[96,576]{1,0:T(8,128)} %param.19) | copy-start | bytes 663556
  9.2 9.3 %collective-permute-start.2 = (bf16[96,640]{1,0:T(8,128)(2,1)S(1)}, bf16[96,640]{1,0:T(8,128)(2,1)S(1)}, u32[]{:S(2)}, u32[]{:S(2)}) collective-permute-start(bf16[96,640]{1,0:T(8,128)(2,1)S(1)} %maximum_maximum_fusion), channel_id=1, source_target_pairs={{0,3},{1,2},{2,1},{3,0},{4,7},{5,6},{6,5},{7,4},{8,11},{9,10},{10,... | collective-permute-start | bytes 368648 | tf_op jit(solution)/shard_map/ppermute | solution.py:341
  14.3 10.4 %collective-permute-start.1 = (bf16[96,640]{1,0:T(8,128)(2,1)S(1)}, bf16[96,640]{1,0:T(8,128)(2,1)S(1)}, u32[]{:S(2)}, u32[]{:S(2)}) collective-permute-start(bf16[96,640]{1,0:T(8,128)(2,1)S(1)} %maximum_maximum_fusion), channel_id=1, source_target_pairs={{0,2},{1,3},{2,0},{3,1},{4,6},{5,7},{6,4},{7,5},{8,10},{9,11},{10,... | collective-permute-start | bytes 368648 | tf_op jit(solution)/shard_map/ppermute | solution.py:341
  14.3 11.0 %collective-permute-start = (bf16[96,640]{1,0:T(8,128)(2,1)S(1)}, bf16[96,640]{1,0:T(8,128)(2,1)S(1)}, u32[]{:S(2)}, u32[]{:S(2)}) collective-permute-start(bf16[96,640]{1,0:T(8,128)(2,1)S(1)} %maximum_maximum_fusion), channel_id=1, source_target_pairs={{0,1},{1,0},{2,3},{3,2},{4,5},{5,4},{6,7},{7,6},{8,9},{9,8},{10,11... | collective-permute-start | bytes 368648 | tf_op jit(solution)/shard_map/ppermute | solution.py:341
  26.2 24.4 %copy-start.1 = (bf16[4,96,576]{2,1,0:T(8,128)(2,1)}, bf16[4,96,576]{2,1,0:T(8,128)(2,1)S(1)}, u32[]{:S(2)}) copy-start(bf16[4,96,576]{2,1,0:T(8,128)(2,1)S(1)} %pad_maximum_fusion.1.refs_4_) | copy-start | bytes 1327108
  26.2 12.3 %collective-permute-start.4 = (bf16[4,96,576]{2,1,0:T(8,128)(2,1)S(1)}, bf16[4,96,576]{2,1,0:T(8,128)(2,1)S(1)}, u32[]{:S(2)}, u32[]{:S(2)}) collective-permute-start(bf16[4,96,576]{2,1,0:T(8,128)(2,1)S(1)} %pad_maximum_fusion.1.refs_4_), channel_id=1, source_target_pairs={{0,16},{4,20},{8,24},{12,28},{16,0},{20,4},{24,8},{28,12},{1,17},{... | collective-permute-start | bytes 1327112 | tf_op jit(solution)/shard_map/ppermute | solution.py:341
  27.8 12.3 %collective-permute-start.3 = (bf16[4,96,576]{2,1,0:T(8,128)(2,1)S(1)}, bf16[4,96,576]{2,1,0:T(8,128)(2,1)S(1)}, u32[]{:S(2)}, u32[]{:S(2)}) collective-permute-start(bf16[4,96,576]{2,1,0:T(8,128)(2,1)S(1)} %pad_maximum_fusion.1.refs_4_), channel_id=1, source_target_pairs={{0,8},{4,12},{8,0},{12,4},{16,24},{20,28},{24,16},{28,20},{1,9},{5... | collective-permute-start | bytes 1327112 | tf_op jit(solution)/shard_map/ppermute | solution.py:341
  29.3 20.1 %collective-permute-start.7 = (bf16[4,96,576]{2,1,0:T(8,128)(2,1)S(1)}, bf16[4,96,576]{2,1,0:T(8,128)(2,1)S(1)}, u32[]{:S(2)}, u32[]{:S(2)}) collective-permute-start(bf16[4,96,576]{2,1,0:T(8,128)(2,1)S(1)} %pad_maximum_fusion.1.refs_4_), channel_id=1, source_target_pairs={{0,4},{4,0},{8,12},{12,8},{16,20},{20,16},{24,28},{28,24},{1,5},{5... | collective-permute-start | bytes 1327112 | tf_op jit(solution)/shard_map/ppermute | solution.py:341
  38.6 6.6 %collective-permute-start.6 = (bf16[2,96,576]{2,1,0:T(8,128)(2,1)S(1)}, bf16[2,96,576]{2,1,0:T(8,128)(2,1)}, u32[]{:S(2)}, u32[]{:S(2)}) collective-permute-start(bf16[2,96,576]{2,1,0:T(8,128)(2,1)S(1)} %slice.127), channel_id=1, source_target_pairs={{0,8},{4,12},{8,0},{12,4},{16,24},{20,28},{24,16},{28,20},{1,9},{5... | collective-permute-start | bytes 663560 | tf_op jit(solution)/shard_map/ppermute | solution.py:341
  40.2 9.3 %collective-permute-start.9 = (bf16[4,96,576]{2,1,0:T(8,128)(2,1)S(1)}, bf16[4,96,576]{2,1,0:T(8,128)(2,1)S(1)}, u32[]{:S(2)}, u32[]{:S(2)}) collective-permute-start(bf16[4,96,576]{2,1,0:T(8,128)(2,1)S(1)} %collective-permute-done.4.refs_6_), channel_id=1, source_target_pairs={{0,4},{4,0},{8,12},{12,8},{16,20},{20,16},{24,28},{28,24},{1,5},{5... | collective-permute-start | bytes 1327112 | tf_op jit(solution)/shard_map/ppermute | solution.py:341
  40.2 8.5 %collective-permute-start.5 = (bf16[2,96,576]{2,1,0:T(8,128)(2,1)S(1)}, bf16[2,96,576]{2,1,0:T(8,128)(2,1)}, u32[]{:S(2)}, u32[]{:S(2)}) collective-permute-start(bf16[2,96,576]{2,1,0:T(8,128)(2,1)S(1)} %slice.126), channel_id=1, source_target_pairs={{0,16},{4,20},{8,24},{12,28},{16,0},{20,4},{24,8},{28,12},{1,17},{... | collective-permute-start | bytes 663560 | tf_op jit(solution)/shard_map/ppermute | solution.py:341
  41.8 8.8 %collective-permute-start.8 = (bf16[4,96,576]{2,1,0:T(8,128)(2,1)S(1)}, bf16[4,96,576]{2,1,0:T(8,128)(2,1)S(1)}, u32[]{:S(2)}, u32[]{:S(2)}) collective-permute-start(bf16[4,96,576]{2,1,0:T(8,128)(2,1)S(1)} %collective-permute-done.3.refs_5_), channel_id=1, source_target_pairs={{0,4},{4,0},{8,12},{12,8},{16,20},{20,16},{24,28},{28,24},{1,5},{5... | collective-permute-start | bytes 1327112 | tf_op jit(solution)/shard_map/ppermute | solution.py:341
  45.2 4.2 %collective-permute-start.11 = (bf16[2,96,576]{2,1,0:T(8,128)(2,1)}, bf16[2,96,576]{2,1,0:T(8,128)(2,1)}, u32[]{:S(2)}, u32[]{:S(2)}) collective-permute-start(bf16[2,96,576]{2,1,0:T(8,128)(2,1)} %collective-permute-done.6.refs_8_), channel_id=1, source_target_pairs={{0,4},{4,0},{8,12},{12,8},{16,20},{20,16},{24,28},{28,24},{1,5},{5... | collective-permute-start | bytes 663560 | tf_op jit(solution)/shard_map/ppermute | solution.py:341
  48.7 1.9 collective-permute-start.10
  60.1 31.4 %collective-permute-start.16 = (bf16[4,96,1792]{2,1,0:T(8,128)(2,1)}, bf16[4,96,1792]{2,1,0:T(8,128)(2,1)S(1)}, u32[]{:S(2)}, u32[]{:S(2)}) collective-permute-start(bf16[4,96,1792]{2,1,0:T(8,128)(2,1)} %bitcast.65), channel_id=1, source_target_pairs={{0,16},{4,20},{8,24},{12,28},{16,0},{20,4},{24,8},{28,12},{1,17},{... | collective-permute-start | bytes 4128776 | tf_op jit(solution)/shard_map/ppermute | solution.py:341
  61.6 31.1 %collective-permute-start.15 = (bf16[4,96,1792]{2,1,0:T(8,128)(2,1)}, bf16[4,96,1792]{2,1,0:T(8,128)(2,1)S(1)}, u32[]{:S(2)}, u32[]{:S(2)}) collective-permute-start(bf16[4,96,1792]{2,1,0:T(8,128)(2,1)} %bitcast.66), channel_id=1, source_target_pairs={{0,8},{4,12},{8,0},{12,4},{16,24},{20,28},{24,16},{28,20},{1,9},{5... | collective-permute-start | bytes 4128776 | tf_op jit(solution)/shard_map/ppermute | solution.py:341
  63.1 12.8 %collective-permute-start.12 = (bf16[1152,128]{1,0:T(8,128)(2,1)}, bf16[1152,128]{1,0:T(8,128)(2,1)S(1)}, u32[]{:S(2)}, u32[]{:S(2)}) collective-permute-start(bf16[1152,128]{1,0:T(8,128)(2,1)} %get-tuple-element.115), channel_id=1, source_target_pairs={{0,1},{1,0},{2,3},{3,2},{4,5},{5,4},{6,7},{7,6},{8,9},{9,8},{10,11... | collective-permute-start | bytes 884744 | tf_op jit(solution)/shard_map/ppermute | solution.py:341
  63.7 23.7 %collective-permute-start.13 = (bf16[1152,128]{1,0:T(8,128)(2,1)}, bf16[1152,128]{1,0:T(8,128)(2,1)S(1)}, u32[]{:S(2)}, u32[]{:S(2)}) collective-permute-start(bf16[1152,128]{1,0:T(8,128)(2,1)} %get-tuple-element.116), channel_id=1, source_target_pairs={{0,2},{1,3},{2,0},{3,1},{4,6},{5,7},{6,4},{7,5},{8,10},{9,11},{10,... | collective-permute-start | bytes 884744 | tf_op jit(solution)/shard_map/ppermute | solution.py:341
  65.0 22.5 %collective-permute-start.14 = (bf16[1152,128]{1,0:T(8,128)(2,1)}, bf16[1152,128]{1,0:T(8,128)(2,1)S(1)}, u32[]{:S(2)}, u32[]{:S(2)}) collective-permute-start(bf16[1152,128]{1,0:T(8,128)(2,1)} %get-tuple-element.117), channel_id=1, source_target_pairs={{0,3},{1,2},{2,1},{3,0},{4,7},{5,6},{6,5},{7,4},{8,11},{9,10},{10,... | collective-permute-start | bytes 884744 | tf_op jit(solution)/shard_map/ppermute | solution.py:341
  75.9 21.3 %copy-start.20 = (bf16[1152,128]{1,0:T(8,128)(2,1)}, bf16[1152,128]{1,0:T(8,128)(2,1)S(1)}, u32[]{:S(2)}) copy-start(bf16[1152,128]{1,0:T(8,128)(2,1)S(1)} %collective-permute-done.12.refs_1_) | copy-start | bytes 884740
  75.9 27.4 %collective-permute-start.19 = (bf16[4,96,1792]{2,1,0:T(8,128)(2,1)}, bf16[4,96,1792]{2,1,0:T(8,128)(2,1)S(1)}, u32[]{:S(2)}, u32[]{:S(2)}) collective-permute-start(bf16[4,96,1792]{2,1,0:T(8,128)(2,1)} %bitcast.67), channel_id=1, source_target_pairs={{0,4},{4,0},{8,12},{12,8},{16,20},{20,16},{24,28},{28,24},{1,5},{5... | collective-permute-start | bytes 4128776 | tf_op jit(solution)/shard_map/ppermute | solution.py:341
  92.8 10.5 %collective-permute-start.20 = (bf16[4,96,1792]{2,1,0:T(8,128)(2,1)S(1)}, bf16[4,96,1792]{2,1,0:T(8,128)(2,1)S(1)}, u32[]{:S(2)}, u32[]{:S(2)}) collective-permute-start(bf16[4,96,1792]{2,1,0:T(8,128)(2,1)S(1)} %collective-permute-done.15.refs_9_), channel_id=1, source_target_pairs={{0,4},{4,0},{8,12},{12,8},{16,20},{20,16},{24,28},{28,24},{1,5},{5... | collective-permute-start | bytes 4128776 | tf_op jit(solution)/shard_map/ppermute | solution.py:341
  92.8 10.5 %collective-permute-start.21 = (bf16[4,96,1792]{2,1,0:T(8,128)(2,1)S(1)}, bf16[4,96,1792]{2,1,0:T(8,128)(2,1)S(1)}, u32[]{:S(2)}, u32[]{:S(2)}) collective-permute-start(bf16[4,96,1792]{2,1,0:T(8,128)(2,1)S(1)} %collective-permute-done.16.refs_10_), channel_id=1, source_target_pairs={{0,4},{4,0},{8,12},{12,8},{16,20},{20,16},{24,28},{28,24},{1,5},{5... | collective-permute-start | bytes 4128776 | tf_op jit(solution)/shard_map/ppermute | solution.py:341
  95.1 17.7 %collective-permute-start.18 = (bf16[2,96,1792]{2,1,0:T(8,128)(2,1)}, bf16[2,96,1792]{2,1,0:T(8,128)(2,1)}, u32[]{:S(2)}, u32[]{:S(2)}) collective-permute-start(bf16[2,96,1792]{2,1,0:T(8,128)(2,1)} %slice.104), channel_id=1, source_target_pairs={{0,8},{4,12},{8,0},{12,4},{16,24},{20,28},{24,16},{28,20},{1,9},{5... | collective-permute-start | bytes 2064392 | tf_op jit(solution)/shard_map/ppermute | solution.py:341
  96.5 17.4 %collective-permute-start.17 = (bf16[2,96,1792]{2,1,0:T(8,128)(2,1)}, bf16[2,96,1792]{2,1,0:T(8,128)(2,1)}, u32[]{:S(2)}, u32[]{:S(2)}) collective-permute-start(bf16[2,96,1792]{2,1,0:T(8,128)(2,1)} %slice.103), channel_id=1, source_target_pairs={{0,16},{4,20},{8,24},{12,28},{16,0},{20,4},{24,8},{28,12},{1,17},{... | collective-permute-start | bytes 2064392 | tf_op jit(solution)/shard_map/ppermute | solution.py:341
  103.3 14.9 %copy-start.11 = (bf16[4,96,1792]{2,1,0:T(8,128)(2,1)}, bf16[4,96,1792]{2,1,0:T(8,128)(2,1)S(1)}, u32[]{:S(2)}) copy-start(bf16[4,96,1792]{2,1,0:T(8,128)(2,1)S(1)} %collective-permute-done.19.refs_13_) | copy-start | bytes 4128772
  103.3 10.7 %collective-permute-start.22 = (bf16[384,128]{1,0:T(8,128)(2,1)}, bf16[384,128]{1,0:T(8,128)(2,1)S(1)}, u32[]{:S(2)}, u32[]{:S(2)}) collective-permute-start(bf16[384,128]{1,0:T(8,128)(2,1)} %get-tuple-element.129), channel_id=1, source_target_pairs={{0,1},{1,0},{2,3},{3,2},{4,5},{5,4},{6,7},{7,6},{8,9},{9,8},{10,11... | collective-permute-start | bytes 294920 | tf_op jit(solution)/shard_map/ppermute | solution.py:341
  104.5 10.2 %collective-permute-start.23 = (bf16[384,128]{1,0:T(8,128)(2,1)}, bf16[384,128]{1,0:T(8,128)(2,1)S(1)}, u32[]{:S(2)}, u32[]{:S(2)}) collective-permute-start(bf16[384,128]{1,0:T(8,128)(2,1)} %get-tuple-element.130), channel_id=1, source_target_pairs={{0,2},{1,3},{2,0},{3,1},{4,6},{5,7},{6,4},{7,5},{8,10},{9,11},{10,... | collective-permute-start | bytes 294920 | tf_op jit(solution)/shard_map/ppermute | solution.py:341
  106.2 8.6 %collective-permute-start.24 = (bf16[384,128]{1,0:T(8,128)(2,1)}, bf16[384,128]{1,0:T(8,128)(2,1)S(1)}, u32[]{:S(2)}, u32[]{:S(2)}) collective-permute-start(bf16[384,128]{1,0:T(8,128)(2,1)} %get-tuple-element.131), channel_id=1, source_target_pairs={{0,3},{1,2},{2,1},{3,0},{4,7},{5,6},{6,5},{7,4},{8,11},{9,10},{10,... | collective-permute-start | bytes 294920 | tf_op jit(solution)/shard_map/ppermute | solution.py:341
  114.8 2.4 collective-permute-start.25
  114.9 3.3 %collective-permute-start.26 = (bf16[2,96,1792]{2,1,0:T(8,128)(2,1)}, bf16[2,96,1792]{2,1,0:T(8,128)(2,1)S(1)}, u32[]{:S(2)}, u32[]{:S(2)}) collective-permute-start(bf16[2,96,1792]{2,1,0:T(8,128)(2,1)} %collective-permute-done.18.refs_12_), channel_id=1, source_target_pairs={{0,4},{4,0},{8,12},{12,8},{16,20},{20,16},{24,28},{28,24},{1,5},{5... | collective-permute-start | bytes 2064392 | tf_op jit(solution)/shard_map/ppermute | solution.py:341
  137.0 7.6 %collective-permute-start.27 = (bf16[9,256,768]{2,1,0:T(8,128)(2,1)}, bf16[9,256,768]{2,1,0:T(8,128)(2,1)S(1)}, u32[]{:S(2)}, u32[]{:S(2)}) collective-permute-start(bf16[9,256,768]{2,1,0:T(8,128)(2,1)} %get-tuple-element.143.refs_2_.refs_0_), channel_id=1, source_target_pairs={{0,4},{4,0},{8,12},{12,8},{16,20},{20,16},{24,28},{28,24},{1,5},{5... | collective-permute-start | bytes 10616840 | tf_op jit(solution)/shard_map/ppermute | solution.py:341
  137.2 7.4 %collective-permute-start.28 = (bf16[4,256,384]{2,1,0:T(8,128)(2,1)}, bf16[4,256,384]{2,1,0:T(8,128)(2,1)S(1)}, u32[]{:S(2)}, u32[]{:S(2)}) collective-permute-start(bf16[4,256,384]{2,1,0:T(8,128)(2,1)} %get-tuple-element.145), channel_id=1, source_target_pairs={{0,4},{4,0},{8,12},{12,8},{16,20},{20,16},{24,28},{28,24},{1,5},{5... | collective-permute-start | bytes 2359304 | tf_op jit(solution)/shard_map/ppermute | solution.py:341
  137.6 19.1 %collective-permute-start.29 = (bf16[384,128]{1,0:T(8,128)(2,1)}, bf16[384,128]{1,0:T(8,128)(2,1)S(1)}, u32[]{:S(2)}, u32[]{:S(2)}) collective-permute-start(bf16[384,128]{1,0:T(8,128)(2,1)} %get-tuple-element.151), channel_id=1, source_target_pairs={{0,1},{1,0},{2,3},{3,2},{4,5},{5,4},{6,7},{7,6},{8,9},{9,8},{10,11... | collective-permute-start | bytes 294920 | tf_op jit(solution)/shard_map/ppermute | solution.py:341
  139.2 17.6 %collective-permute-start.30 = (bf16[384,128]{1,0:T(8,128)(2,1)}, bf16[384,128]{1,0:T(8,128)(2,1)S(1)}, u32[]{:S(2)}, u32[]{:S(2)}) collective-permute-start(bf16[384,128]{1,0:T(8,128)(2,1)} %get-tuple-element.152), channel_id=1, source_target_pairs={{0,2},{1,3},{2,0},{3,1},{4,6},{5,7},{6,4},{7,5},{8,10},{9,11},{10,... | collective-permute-start | bytes 294920 | tf_op jit(solution)/shard_map/ppermute | solution.py:341
  140.4 16.3 %collective-permute-start.31 = (bf16[384,128]{1,0:T(8,128)(2,1)}, bf16[384,128]{1,0:T(8,128)(2,1)S(1)}, u32[]{:S(2)}, u32[]{:S(2)}) collective-permute-start(bf16[384,128]{1,0:T(8,128)(2,1)} %get-tuple-element.153), channel_id=1, source_target_pairs={{0,3},{1,2},{2,1},{3,0},{4,7},{5,6},{6,5},{7,4},{8,11},{9,10},{10,... | collective-permute-start | bytes 294920 | tf_op jit(solution)/shard_map/ppermute | solution.py:341
  156.8 38.0 %collective-permute-start.33 = (bf16[2,2,96,1792]{3,2,1,0:T(8,128)(2,1)}, bf16[2,2,96,1792]{3,2,1,0:T(8,128)(2,1)S(1)}, u32[]{:S(2)}, u32[]{:S(2)}) collective-permute-start(bf16[2,2,96,1792]{3,2,1,0:T(8,128)(2,1)} %get-tuple-element.159), channel_id=1, source_target_pairs={{0,16},{4,20},{8,24},{12,28},{16,0},{20,4},{24,8},{28,12},{1,17},{... | collective-permute-start | bytes 4128776 | tf_op jit(solution)/shard_map/ppermute | solution.py:341
  158.3 36.4 %collective-permute-start.34 = (bf16[2,2,96,1792]{3,2,1,0:T(8,128)(2,1)}, bf16[2,2,96,1792]{3,2,1,0:T(8,128)(2,1)S(1)}, u32[]{:S(2)}, u32[]{:S(2)}) collective-permute-start(bf16[2,2,96,1792]{3,2,1,0:T(8,128)(2,1)} %get-tuple-element.160), channel_id=1, source_target_pairs={{0,8},{4,12},{8,0},{12,4},{16,24},{20,28},{24,16},{28,20},{1,9},{5... | collective-permute-start | bytes 4128776 | tf_op jit(solution)/shard_map/ppermute | solution.py:341
  180.6 14.1 %collective-permute-start.35 = (bf16[1152,128]{1,0:T(8,128)(2,1)}, bf16[1152,128]{1,0:T(8,128)(2,1)S(1)}, u32[]{:S(2)}, u32[]{:S(2)}) collective-permute-start(bf16[1152,128]{1,0:T(8,128)(2,1)} %get-tuple-element.161), channel_id=1, source_target_pairs={{0,1},{1,0},{2,3},{3,2},{4,5},{5,4},{6,7},{7,6},{8,9},{9,8},{10,11... | collective-permute-start | bytes 884744 | tf_op jit(solution)/shard_map/ppermute | solution.py:341
  182.2 23.7 %collective-permute-start.36 = (bf16[1152,128]{1,0:T(8,128)(2,1)}, bf16[1152,128]{1,0:T(8,128)(2,1)S(1)}, u32[]{:S(2)}, u32[]{:S(2)}) collective-permute-start(bf16[1152,128]{1,0:T(8,128)(2,1)} %get-tuple-element.168), channel_id=1, source_target_pairs={{0,2},{1,3},{2,0},{3,1},{4,6},{5,7},{6,4},{7,5},{8,10},{9,11},{10,... | collective-permute-start | bytes 884744 | tf_op jit(solution)/shard_map/ppermute | solution.py:341
  183.5 22.4 %collective-permute-start.37 = (bf16[1152,128]{1,0:T(8,128)(2,1)}, bf16[1152,128]{1,0:T(8,128)(2,1)S(1)}, u32[]{:S(2)}, u32[]{:S(2)}) collective-permute-start(bf16[1152,128]{1,0:T(8,128)(2,1)} %get-tuple-element.169), channel_id=1, source_target_pairs={{0,3},{1,2},{2,1},{3,0},{4,7},{5,6},{6,5},{7,4},{8,11},{9,10},{10,... | collective-permute-start | bytes 884744 | tf_op jit(solution)/shard_map/ppermute | solution.py:341
  206.0 3.8 %collective-permute-start.38 = (bf16[3,1152,128]{2,1,0:T(8,128)(2,1)S(1)}, bf16[3,1152,128]{2,1,0:T(8,128)(2,1)S(1)}, u32[]{:S(2)}, u32[]{:S(2)}) collective-permute-start(bf16[3,1152,128]{2,1,0:T(8,128)(2,1)S(1)} %pad_maximum_fusion.refs_4_), channel_id=1, source_target_pairs={{0,4},{4,0},{8,12},{12,8},{16,20},{20,16},{24,28},{28,24},{1,5},{5... | collective-permute-start | bytes 2654216 | tf_op jit(solution)/shard_map/ppermute | solution.py:341
  206.1 17.8 %collective-permute-start.39 = (bf16[2,96,1792]{2,1,0:T(8,128)(2,1)S(1)}, bf16[2,96,1792]{2,1,0:T(8,128)(2,1)S(1)}, u32[]{:S(2)}, u32[]{:S(2)}) collective-permute-start(bf16[2,96,1792]{2,1,0:T(8,128)(2,1)S(1)} %copy-done.50), channel_id=1, source_target_pairs={{0,8},{4,12},{8,0},{12,4},{16,24},{20,28},{24,16},{28,20},{1,9},{5... | collective-permute-start | bytes 2064392 | tf_op jit(solution)/shard_map/ppermute | solution.py:341
  207.6 17.5 %collective-permute-start.40 = (bf16[2,96,1792]{2,1,0:T(8,128)(2,1)S(1)}, bf16[2,96,1792]{2,1,0:T(8,128)(2,1)S(1)}, u32[]{:S(2)}, u32[]{:S(2)}) collective-permute-start(bf16[2,96,1792]{2,1,0:T(8,128)(2,1)S(1)} %copy-done.49), channel_id=1, source_target_pairs={{0,16},{4,20},{8,24},{12,28},{16,0},{20,4},{24,8},{28,12},{1,17},{... | collective-permute-start | bytes 2064392 | tf_op jit(solution)/shard_map/ppermute | solution.py:341
  208.2 1.6 collective-permute-start.32
  217.9 21.7 %copy-start.27 = (bf16[2,2,96,576]{3,2,1,0:T(8,128)(2,1)S(1)}, bf16[2,2,96,576]{3,2,1,0:T(8,128)(2,1)}, u32[]{:S(2)}) copy-start(bf16[2,2,96,576]{3,2,1,0:T(8,128)(2,1)} %get-tuple-element.189) | copy-start | bytes 1327108
  225.1 12.7 %collective-permute-start.41 = (bf16[2,2,96,576]{3,2,1,0:T(8,128)(2,1)}, bf16[2,2,96,576]{3,2,1,0:T(8,128)(2,1)S(1)}, u32[]{:S(2)}, u32[]{:S(2)}) collective-permute-start(bf16[2,2,96,576]{3,2,1,0:T(8,128)(2,1)} %get-tuple-element.188), channel_id=1, source_target_pairs={{0,16},{4,20},{8,24},{12,28},{16,0},{20,4},{24,8},{28,12},{1,17},{... | collective-permute-start | bytes 1327112 | tf_op jit(solution)/shard_map/ppermute | solution.py:341
  225.7 14.0 %collective-permute-start.43 = (bf16[2,2,96,576]{3,2,1,0:T(8,128)(2,1)}, bf16[2,2,96,576]{3,2,1,0:T(8,128)(2,1)S(1)}, u32[]{:S(2)}, u32[]{:S(2)}) collective-permute-start(bf16[2,2,96,576]{3,2,1,0:T(8,128)(2,1)} %get-tuple-element.190), channel_id=1, source_target_pairs={{0,8},{4,12},{8,0},{12,4},{16,24},{20,28},{24,16},{28,20},{1,9},{5... | collective-permute-start | bytes 1327112 | tf_op jit(solution)/shard_map/ppermute | solution.py:341
  239.0 13.8 %collective-permute-start.42 = (bf16[2,96,576]{2,1,0:T(8,128)(2,1)S(1)}, bf16[2,96,576]{2,1,0:T(8,128)(2,1)S(1)}, u32[]{:S(2)}, u32[]{:S(2)}) collective-permute-start(bf16[2,96,576]{2,1,0:T(8,128)(2,1)S(1)} %fusion.9), channel_id=1, source_target_pairs={{0,8},{4,12},{8,0},{12,4},{16,24},{20,28},{24,16},{28,20},{1,9},{5... | collective-permute-start | bytes 663560 | tf_op jit(solution)/shard_map/ppermute | solution.py:341
  239.8 13.0 %collective-permute-start.44 = (bf16[2,96,576]{2,1,0:T(8,128)(2,1)S(1)}, bf16[2,96,576]{2,1,0:T(8,128)(2,1)S(1)}, u32[]{:S(2)}, u32[]{:S(2)}) collective-permute-start(bf16[2,96,576]{2,1,0:T(8,128)(2,1)S(1)} %fusion.10), channel_id=1, source_target_pairs={{0,16},{4,20},{8,24},{12,28},{16,0},{20,4},{24,8},{28,12},{1,17},{... | collective-permute-start | bytes 663560 | tf_op jit(solution)/shard_map/ppermute | solution.py:341
  240.5 25.2 %collective-permute-start.47 = (bf16[2,96,1792]{2,1,0:T(8,128)(2,1)S(1)}, bf16[2,96,1792]{2,1,0:T(8,128)(2,1)S(1)}, u32[]{:S(2)}, u32[]{:S(2)}) collective-permute-start(bf16[2,96,1792]{2,1,0:T(8,128)(2,1)S(1)} %add_convert_fusion), channel_id=1, source_target_pairs={{0,1},{1,0},{2,3},{3,2},{4,5},{5,4},{6,7},{7,6},{8,9},{9,8},{10,11... | collective-permute-start | bytes 2064392 | tf_op jit(solution)/shard_map/ppermute | solution.py:341
  245.8 19.9 %copy-start.14 = (f32[2,96,1792]{2,1,0:T(8,128)S(1)}, f32[2,96,1792]{2,1,0:T(8,128)}, u32[]{:S(2)}) copy-start(f32[2,96,1792]{2,1,0:T(8,128)} %get-tuple-element.197) | copy-start | bytes 4128772
  252.8 7.7 %collective-permute-start.49 = (f32[16,192]{1,0:T(8,128)}, f32[16,192]{1,0:T(8,128)S(1)}, u32[]{:S(2)}, u32[]{:S(2)}) collective-permute-start(f32[16,192]{1,0:T(8,128)} %get-tuple-element.202), channel_id=1, source_target_pairs={{0,1},{1,0},{2,3},{3,2},{4,5},{5,4},{6,7},{7,6},{8,9},{9,8},{10,11... | collective-permute-start | bytes 36872 | tf_op jit(solution)/shard_map/ppermute | solution.py:341
  252.9 7.6 %collective-permute-start.50 = (f32[16,192]{1,0:T(8,128)}, f32[16,192]{1,0:T(8,128)S(1)}, u32[]{:S(2)}, u32[]{:S(2)}) collective-permute-start(f32[16,192]{1,0:T(8,128)} %get-tuple-element.203), channel_id=1, source_target_pairs={{0,2},{1,3},{2,0},{3,1},{4,6},{5,7},{6,4},{7,5},{8,10},{9,11},{10,... | collective-permute-start | bytes 36872 | tf_op jit(solution)/shard_map/ppermute | solution.py:341
  255.8 7.0 %collective-permute-start.51 = (f32[16,192]{1,0:T(8,128)}, f32[16,192]{1,0:T(8,128)S(1)}, u32[]{:S(2)}, u32[]{:S(2)}) collective-permute-start(f32[16,192]{1,0:T(8,128)} %get-tuple-element.204), channel_id=1, source_target_pairs={{0,3},{1,2},{2,1},{3,0},{4,7},{5,6},{6,5},{7,4},{8,11},{9,10},{10,... | collective-permute-start | bytes 36872 | tf_op jit(solution)/shard_map/ppermute | solution.py:341
  263.5 1.2 collective-permute-start.52
  263.6 10.8 %collective-permute-start.45 = (bf16[2,96,576]{2,1,0:T(8,128)(2,1)S(1)}, bf16[2,96,576]{2,1,0:T(8,128)(2,1)S(1)}, u32[]{:S(2)}, u32[]{:S(2)}) collective-permute-start(bf16[2,96,576]{2,1,0:T(8,128)(2,1)S(1)} %fusion.2), channel_id=1, source_target_pairs={{0,1},{1,0},{2,3},{3,2},{4,5},{5,4},{6,7},{7,6},{8,9},{9,8},{10,11... | collective-permute-start | bytes 663560 | tf_op jit(solution)/shard_map/ppermute | solution.py:341
  264.7 3.7 %collective-permute-start.53 = (f32[16,192]{1,0:T(8,128)S(1)}, f32[16,192]{1,0:T(8,128)S(1)}, u32[]{:S(2)}, u32[]{:S(2)}) collective-permute-start(f32[16,192]{1,0:T(8,128)S(1)} %add.158), channel_id=1, source_target_pairs={{0,8},{4,12},{8,0},{12,4},{16,24},{20,28},{24,16},{28,20},{1,9},{5... | collective-permute-start | bytes 36872 | tf_op jit(solution)/shard_map/ppermute | solution.py:341
  265.9 23.6 %copy-start.36 = (f32[96,576]{1,0:T(8,128)S(1)}, f32[96,576]{1,0:T(8,128)}, u32[]{:S(2)}) copy-start(f32[96,576]{1,0:T(8,128)} %param.25) | copy-start | bytes 663556
  265.9 23.6 %copy-start.37 = (f32[96,576]{1,0:T(8,128)S(1)}, f32[96,576]{1,0:T(8,128)}, u32[]{:S(2)}) copy-start(f32[96,576]{1,0:T(8,128)} %param.24) | copy-start | bytes 663556
  266.0 24.5 %collective-permute-start.48 = (bf16[96,1792]{1,0:T(8,128)(2,1)S(1)}, bf16[96,1792]{1,0:T(8,128)(2,1)S(1)}, u32[]{:S(2)}, u32[]{:S(2)}) collective-permute-start(bf16[96,1792]{1,0:T(8,128)(2,1)S(1)} %fusion.5), channel_id=1, source_target_pairs={{0,2},{1,3},{2,0},{3,1},{4,6},{5,7},{6,4},{7,5},{8,10},{9,11},{10,... | collective-permute-start | bytes 1032200 | tf_op jit(solution)/shard_map/ppermute | solution.py:341
  268.4 6.6 %collective-permute-start.54 = (f32[16,192]{1,0:T(8,128)S(1)}, f32[16,192]{1,0:T(8,128)S(1)}, u32[]{:S(2)}, u32[]{:S(2)}) collective-permute-start(f32[16,192]{1,0:T(8,128)S(1)} %add.159), channel_id=1, source_target_pairs={{0,16},{4,20},{8,24},{12,28},{16,0},{20,4},{24,8},{28,12},{1,17},{... | collective-permute-start | bytes 36872 | tf_op jit(solution)/shard_map/ppermute | solution.py:341
  274.5 15.0 %collective-permute-start.46 = (bf16[96,576]{1,0:T(8,128)(2,1)S(1)}, bf16[96,576]{1,0:T(8,128)(2,1)S(1)}, u32[]{:S(2)}, u32[]{:S(2)}) collective-permute-start(bf16[96,576]{1,0:T(8,128)(2,1)S(1)} %fusion.12), channel_id=1, source_target_pairs={{0,2},{1,3},{2,0},{3,1},{4,6},{5,7},{6,4},{7,5},{8,10},{9,11},{10,... | collective-permute-start | bytes 331784 | tf_op jit(solution)/shard_map/ppermute | solution.py:341
  (43 other events, 181.0 us)
Sparse Core Ops, SparseCore 0:
  26.1 33.9 all-gather.2
where the time goes:
time: 306 us; the launch traced here: 301 us
  waiting for transfers between devices  125 us (41%)
  Pallas kernels  80.3 us (26%)
  starting transfers between devices  57 us (19%)
  between operations  14.9 us (5%)
  local copies, waits for them, and re-layouts  13.4 us (4%)
  other arithmetic  11.2 us (4%)
    ppermute x55, waiting for transfers between devices, swap(): return lax.ppermute(value, axis, [(i, i ^ bit) for i in range(size)])  122 us
    pallas_call x8, Pallas kernels, call(): pl.pallas_call(kernel, grid=(1,), out_shape=tuple(outputs), in_specs=[spe...  80.3 us
    ppermute x55, starting transfers between devices, swap(): return lax.ppermute(value, axis, [(i, i ^ bit) for i in range(size)])  57 us
    unnamed x102, local copies, waits for them, and re-layouts  8.38 us
  transfers between devices with their start and end apart: 56, of which 29 were waited for; matrix products, arithmetic and copies ran while one was open for 4% of the time, Pallas kernels for 21%

commit v1 on v0

--- a/solution.py
+++ b/solution.py
@@ -318,8 +318,7 @@
 LOW = jnp.bfloat16
 WIDE = jnp.float32
 CORE, XBIT, YBIT = 1, 2, 4
-PLACES = (0, 1, 2, 3)
-DIFFERENCES = (0, 2, 1, 3)
+PLACES = (0, 2, 1, 3)
 SOURCES = (
     (0, PLACES),
     (XBIT, PLACES),
@@ -371,10 +370,6 @@
     return inverse * (part - mean - normed * cross)
 
 
-def exchange(value):
-    return swap(value, "ctx", 1), swap(value, "ctx", 2), swap(value, "ctx", 3)
-
-
 def gather_first(own):
     return swap(own, "batch", XBIT), swap(own, "batch", YBIT)
 
@@ -425,11 +420,11 @@
     ]
 
 
-def load_weight(meta, parts, place, sems, shift):
+def load_weight(meta, parts, place, sems):
     copies = []
     for part, (source, places) in zip(parts, SOURCES):
         for index, ctx in enumerate(places):
-            ranges = place(meta[0] ^ source, shift ^ ctx)
+            ranges = place(meta[0] ^ source, meta[1] ^ ctx)
             copies.append([(part.at[index, :, lanes], target) for lanes, target in ranges])
     started = []
     for kind in range(len(copies[0])):
@@ -446,7 +441,7 @@
     copies = []
     for y in range(2):
         for x in range(2):
-            for index, ctx in enumerate(DIFFERENCES):
+            for index, ctx in enumerate(PLACES):
                 if index < 2:
                     target = (one_sent if y else one_kept).at[x, index]
                 else:
@@ -515,7 +510,7 @@
 def qkv_kernel(meta, x_ref, *refs):
     vectors, parts, refs = refs[:4], refs[4 : 4 + PARTS], refs[4 + PARTS :]
     h_ref, own, near, far, last, held, units, chunks, sems = refs
-    (copies,) = load_weight(meta, parts, functools.partial(qkv_place, held), sems, meta[1])
+    (copies,) = load_weight(meta, parts, functools.partial(qkv_place, held), sems)
     params = read_vectors(meta, vectors, chunks)
     bias = jnp.concatenate([params[4:5], jnp.zeros((1, WIDTH), WIDE), params[5:6]], axis=1)
     centred, inverse = moments(x_ref[...].astype(WIDE))
@@ -639,7 +634,7 @@
     results, (rows_ref, dbias_ref), refs = refs[:4], refs[4:6], refs[6:]
     out_parts, held_out, held_fc, held_proj, units, total, back, chunks, bias, acts, sems = refs
     place = functools.partial(mlp_place, out_parts, held_fc, held_proj)
-    copies = load_weight(meta, parts, place, sems, 0)
+    copies = load_weight(meta, parts, place, sems)
     vec = read_vectors(meta, vectors, chunks)
     for chunk in range(CTX):
         bias[chunk] = vec[8 + chunk : 9 + chunk]
@@ -767,7 +762,7 @@
 def input_grad_kernel(meta, x_ref, dmid_ref, mixed_ref, rows_ref, dfc_ref, dqkv_ref, *refs):
     vectors, parts, refs = refs[:4], refs[4 : 4 + PARTS], refs[4 + PARTS :]
     grad_ref, results, (held, chunks, rows, sums, sems) = refs[0], refs[1:5], refs[5:]
-    (copies,) = load_weight(meta, parts, functools.partial(qkv_place, held), sems, meta[1])
+    (copies,) = load_weight(meta, parts, functools.partial(qkv_place, held), sems)
     params = read_vectors(meta, vectors, chunks)
     centred, inverse = moments(x_ref[...].astype(WIDE))
     normed = centred * inverse
@@ -799,11 +794,16 @@
         send[...] = (kept[1].astype(WIDE) + back[1].astype(WIDE)).astype(LOW)
 
 
+def near_kernel(one_kept, one_back, two_kept, two_back, one_keep, two_send):
+    one_keep[...] = one_kept[...] + one_back[...].astype(WIDE)
+    two_send[...] = (two_kept[...] + two_back[...].astype(WIDE)).astype(LOW)
+
+
 def shape_of(dtype, *dims):
     return jax.ShapeDtypeStruct(dims, dtype)
 
 
-def call(kernel, arguments, kinds, outputs, out_kinds, scratch):
+def call(kernel, arguments, kinds, outputs, out_kinds, scratch, moved=1):
     spec = {
         "v": pl.BlockSpec(memory_space=pltpu.VMEM),
         "s": pl.BlockSpec(memory_space=pltpu.SMEM),
@@ -817,7 +817,7 @@
         in_specs=[spec[kind] for kind in kinds],
         out_specs=tuple(spec[kind] for kind in out_kinds),
         scratch_shapes=scratch,
-        cost_estimate=pl.CostEstimate(flops=1, bytes_accessed=1, transcendentals=0),
+        cost_estimate=pl.CostEstimate(flops=1, bytes_accessed=moved, transcendentals=0),
         compiler_params=pltpu.CompilerParams(vmem_limit_bytes=VMEM_LIMIT),
     )(*arguments)
 
@@ -867,13 +867,18 @@
         ],
         axis=1,
     )
-    parts_one = (piece_one,) + exchange(piece_one)
-    vec_parts = [part[:48, 3 * GROUP :] for part in parts_one]
-    own_one = jnp.stack([part[:, : 3 * GROUP] for part in parts_one])
+    near = jnp.stack([piece_one, swap(piece_one, "ctx", 2)])
+    far = swap(near, "ctx", 1)
+    vec_parts = [part[:48, 3 * GROUP :] for part in (near[0], far[0], near[1], far[1])]
+    own_one = jnp.concatenate([near, far], axis=0)[:, :, : 3 * GROUP]
     piece_two, late_vec = tie((piece_two, vec_parts))
-    own_two = lax.all_gather(piece_two, "ctx", axis=0)
+    far = swap(piece_two, "ctx", 2)
     x_one, y_one = gather_first(own_one)
-    parts_one = [own_one, x_one, y_one, *gather_second(x_one, y_one)]
+    across_one = gather_second(x_one, y_one)
+    far, across_one = tie((far, across_one))
+    near = jnp.stack([piece_two, far])
+    far = swap(near, "ctx", 1)
+    parts_one = [own_one, x_one, y_one, *across_one]
     parts_one = parts_one + to_core(parts_one)
 
     packed = shape_of(LOW, TOKENS * 3 * GROUP // LANES, LANES)
@@ -890,7 +895,8 @@
     )
     qkv_pieces = [own] + [swap(part, "ctx", bit) for bit, part in zip((1, 2, 3), sent)]
 
-    own_two, late_h = tie((own_two, h_one))
+    far, late_h = tie((far, h_one))
+    own_two = jnp.concatenate([near, far], axis=0)
     x_two, y_two = gather_first(own_two)
     qkv_pieces, x_two, y_two = tie((qkv_pieces, x_two, y_two))
     across_two = gather_second(x_two, y_two)
@@ -999,8 +1005,6 @@
         ],
     )
     qkv_kept = qkv_parts[0], qkv_parts[2]
-    mlp_back, qkv_parts = tie((mlp_back, qkv_parts))
-    mlp_one, mlp_two = scatter_near((one_keep, two_keep), mlp_back)
     qkv_kept = qkv_parts[0], qkv_parts[2]
     qkv_back = swap_pair((qkv_parts[1], qkv_parts[3]), YBIT, XBIT)
     grad_input, own, *sent = call(
@@ -1010,15 +1014,24 @@
         [shape_of(WIDE, TOKENS, WIDTH)] + [shape_of(WIDE, 16, GROUP)] * 4,
         "v" * 5,
         [qkv_held, vec_held, pltpu.VMEM((16, WIDTH), WIDE), vec_held, qkv_sems],
-    )
+        moved=40_000_000,
+    )
+    mlp_back, own, sent = tie((mlp_back, own, sent))
+    mlp_one, mlp_two = call(
+        near_kernel, (one_keep, mlp_back[0], two_keep, mlp_back[1]), "vvvv", pair, "vv", []
+    )
+    mlp_two = swap(mlp_two, "ctx", 1)
     qkv_kept, qkv_sent = scatter_second(qkv_kept, qkv_back)
+    qkv_sent, own, sent = tie((qkv_sent, own, sent))
     qkv_back = swap_pair(qkv_sent, XBIT, YBIT)
-    qkv_back, own, sent = tie((qkv_back, own, sent))
+    vec_grad = own + sum(swap(part, "ctx", bit) for bit, part in zip((1, 2, 3), sent))
+    qkv_back, mlp_two, vec_grad = tie((qkv_back, mlp_two, vec_grad))
+    qkv_one, qkv_two = scatter_near(qkv_kept, qkv_back)
     mlp_grad = scatter_far(mlp_one, mlp_two)
-    qkv_grad = scatter_far(*scatter_near(qkv_kept, qkv_back))
-
-    vec_grad = own + sum(swap(part, "ctx", bit) for bit, part in zip((1, 2, 3), sent))
-    for bit in (CORE, XBIT, YBIT):
+    vec_grad = vec_grad + swap(vec_grad, "batch", CORE)
+    qkv_two, vec_grad = tie((qkv_two, vec_grad))
+    qkv_grad = scatter_far(qkv_one, qkv_two)
+    for bit in (XBIT, YBIT):
         vec_grad = vec_grad + swap(vec_grad, "batch", bit)
     vec_grad = vec_grad[:12]
     fc_grad = mlp_grad[:, :WIDTH]

time: 306 us -> 296 us (0.967)
  between operations: 14.9 us -> 1.61 us
  waiting for transfers between devices: 125 us -> 115 us
  starting transfers between devices: 57 us -> 65.7 us
  Pallas kernels: 80.3 us -> 83.9 us
    ppermute x55 -> x56, starting transfers between devices: 57 us -> 65.7 us  [swap(): return lax.ppermute(value, axis, [(i, i ^ bit) for i in range(size)])]
    ppermute x55 -> x56, waiting for transfers between devices: 122 us -> 115 us  [swap(): return lax.ppermute(value, axis, [(i, i ^ bit) for i in range(size)])]
    pallas_call x8 -> x9, Pallas kernels: 80.3 us -> 83.9 us  [call(): pl.pallas_call(kernel, grid=(1,), out_shape=tuple(outputs), in_specs=[spe...]
    unnamed x102 -> x134, local copies, waits for them, and re-layouts: 8.38 us -> 10.1 us
  transfers between devices with their start and end apart: 56 -> 56, of which waited for: 29 -> 30; matrix products, arithmetic and copies ran while one was open for 4% -> 3% of each run, Pallas kernels for 21% -> 23%
where the time goes in v1:
time: 296 us; the launch traced here: 292 us
  waiting for transfers between devices  115 us (39%)
  Pallas kernels  83.9 us (28%)
  starting transfers between devices  65.7 us (22%)
  local copies, waits for them, and re-layouts  14.4 us (5%)
  other arithmetic  10.7 us (4%)
    ppermute x56, waiting for transfers between devices, swap(): return lax.ppermute(value, axis, [(i, i ^ bit) for i in range(size)])  115 us
    pallas_call x9, Pallas kernels, call(): pl.pallas_call(kernel, grid=(1,), out_shape=tuple(outputs), in_specs=[spe...  83.9 us
    ppermute x56, starting transfers between devices, swap(): return lax.ppermute(value, axis, [(i, i ^ bit) for i in range(size)])  65.7 us
    unnamed x134, local copies, waits for them, and re-layouts  10.1 us
  transfers between devices with their start and end apart: 56, of which 30 were waited for; matrix products, arithmetic and copies ran while one was open for 3% of the time, Pallas kernels for 23%

profile of v1, /device:TPU:0, one launch (start us, length us, event | category | flops | bytes accessed | tf_op | source)
XLA Modules:
  0.0 291.8 jit_solution(13491201459963022095)
XLA Ops:
  2.6 4.1 %collective-permute-start = (bf16[96,640]{1,0:T(8,128)(2,1)S(1)}, bf16[96,640]{1,0:T(8,128)(2,1)S(1)}, u32[]{:S(2)}, u32[]{:S(2)}) collective-permute-start(bf16[96,640]{1,0:T(8,128)(2,1)S(1)} %maximum_maximum_fusion), channel_id=1, source_target_pairs={{0,2},{1,3},{2,0},{3,1},{4,6},{5,7},{6,4},{7,5},{8,10},{9,11},{10,... | collective-permute-start | bytes 368648 | tf_op jit(solution)/shard_map/ppermute | solution.py:340
  6.8 5.9 %collective-permute-done = bf16[96,640]{1,0:T(8,128)(2,1)S(1)} collective-permute-done((bf16[96,640]{1,0:T(8,128)(2,1)S(1)}, bf16[96,640]{1,0:T(8,128)(2,1)S(1)}, u32[]{:S(2)}, u32[]{:S(2)}) %collective-permute-start) | collective-permute-done | bytes 122912 | tf_op jit(solution)/shard_map/ppermute | solution.py:340
  13.7 6.2 %collective-permute-done.1 = bf16[2,96,640]{2,1,0:T(8,128)(2,1)S(1)} collective-permute-done((bf16[2,96,640]{2,1,0:T(8,128)(2,1)S(1)}, bf16[2,96,640]{2,1,0:T(8,128)(2,1)S(1)}, u32[]{:S(2)}, u32[]{:S(2)}) %collective-permute-start.1) | collective-permute-done | bytes 245792 | tf_op jit(solution)/shard_map/ppermute | solution.py:340
  20.0 1.3 collective-permute-start.5
  21.3 1.5 collective-permute-start.3
  25.4 3.3 %collective-permute-start.2 = (bf16[96,1792]{1,0:T(8,128)(2,1)S(1)}, bf16[96,1792]{1,0:T(8,128)(2,1)S(1)}, u32[]{:S(2)}, u32[]{:S(2)}) collective-permute-start(bf16[96,1792]{1,0:T(8,128)(2,1)S(1)} %concatenate.23), channel_id=1, source_target_pairs={{0,2},{1,3},{2,0},{3,1},{4,6},{5,7},{6,4},{7,5},{8,10},{9,11},{10,... | collective-permute-start | bytes 1032200 | tf_op jit(solution)/shard_map/ppermute | solution.py:340
  28.8 2.7 collective-permute-done.5.refs_6_
  31.5 1.3 collective-permute-start.6
  33.4 1.1 collective-permute-start.4
  34.5 8.8 %collective-permute-done.2 = bf16[96,1792]{1,0:T(8,128)(2,1)S(1)} collective-permute-done((bf16[96,1792]{1,0:T(8,128)(2,1)S(1)}, bf16[96,1792]{1,0:T(8,128)(2,1)S(1)}, u32[]{:S(2)}, u32[]{:S(2)}) %collective-permute-start.2) | collective-permute-done | bytes 344096 | tf_op jit(solution)/shard_map/ppermute | solution.py:340
  49.9 6.2 %shard_map.296 = (bf16[256,768]{1,0:T(8,128)(2,1)}, bf16[1152,128]{1,0:T(8,128)(2,1)}, bf16[1152,128]{1,0:T(8,128)(2,1)}, bf16[1152,128]{1,0:T(8,128)(2,1)}, bf16[1152,128]{1,0:T(8,128)(2,1)}) custom-call(s32[2]{0:T(128)} %pad_add_fusion.meta, bf16[256,768]{1,0:T(8,128)(2,1)} %bitcast.62, bf16[48,64]{1,0:T(8,128)(2,1)} %pad_maximum_fusion.6.refs_0_, ...), custom_call_target="tpu_custom_call" | custom-call | flops 1 | bytes 1 | tf_op jit(solution)/shard_map/pallas_call | solution.py:813
  56.1 5.0 %collective-permute-done.7 = bf16[2,96,1792]{2,1,0:T(8,128)(2,1)} collective-permute-done((bf16[2,96,1792]{2,1,0:T(8,128)(2,1)}, bf16[2,96,1792]{2,1,0:T(8,128)(2,1)}, u32[]{:S(2)}, u32[]{:S(2)}) %collective-permute-start.7) | collective-permute-done | bytes 688160 | tf_op jit(solution)/shard_map/ppermute | solution.py:340
  61.1 1.3 pad_maximum_fusion.refs_8_
  63.5 1.6 collective-permute-start.13
  65.1 3.4 %collective-permute-start.14 = (bf16[1152,128]{1,0:T(8,128)(2,1)S(1)}, bf16[1152,128]{1,0:T(8,128)(2,1)S(1)}, u32[]{:S(2)}, u32[]{:S(2)}) collective-permute-start(bf16[1152,128]{1,0:T(8,128)(2,1)S(1)} %copy-done.62), channel_id=1, source_target_pairs={{0,2},{1,3},{2,0},{3,1},{4,6},{5,7},{6,4},{7,5},{8,10},{9,11},{10,... | collective-permute-start | bytes 884744 | tf_op jit(solution)/shard_map/ppermute | solution.py:340
  68.5 7.4 %collective-permute-done.13.refs_1_ = bf16[1152,128]{1,0:T(8,128)(2,1)S(1)} collective-permute-done((bf16[1152,128]{1,0:T(8,128)(2,1)S(1)}, bf16[1152,128]{1,0:T(8,128)(2,1)S(1)}, u32[]{:S(2)}, u32[]{:S(2)}) %collective-permute-start.13) | collective-permute-done | bytes 294944 | tf_op jit(solution)/shard_map/ppermute | solution.py:340
  75.9 13.2 %collective-permute-done.14.refs_2_ = bf16[1152,128]{1,0:T(8,128)(2,1)S(1)} collective-permute-done((bf16[1152,128]{1,0:T(8,128)(2,1)S(1)}, bf16[1152,128]{1,0:T(8,128)(2,1)S(1)}, u32[]{:S(2)}, u32[]{:S(2)}) %collective-permute-start.14) | collective-permute-done | bytes 294944 | tf_op jit(solution)/shard_map/ppermute | solution.py:340
  89.0 3.7 %collective-permute-done.17.refs_10_ = bf16[4,96,1792]{2,1,0:T(8,128)(2,1)S(1)} collective-permute-done((bf16[4,96,1792]{2,1,0:T(8,128)(2,1)S(1)}, bf16[4,96,1792]{2,1,0:T(8,128)(2,1)S(1)}, u32[]{:S(2)}, u32[]{:S(2)}) %collective-permute-start.17) | collective-permute-done | bytes 1376288 | tf_op jit(solution)/shard_map/ppermute | solution.py:340
  95.9 1.4 collective-permute-start.18
  97.4 6.1 %shard_map.297 = (bf16[384,128]{1,0:T(8,128)(2,1)}, bf16[384,128]{1,0:T(8,128)(2,1)}, bf16[384,128]{1,0:T(8,128)(2,1)}, bf16[384,128]{1,0:T(8,128)(2,1)}) custom-call(s32[2]{0:T(128)} %pad_add_fusion.meta, bf16[1152,128]{1,0:T(8,128)(2,1)} %get-tuple-element.135.refs_0_, bf16[1152,128]{1,0:T(8,128)(2,1)} %copy-done.23, bf16[1152,128]{1,0:T(8,128)(2,1)} %copy-done.24, ...), custom_call_target="tpu_custom_call" | custom-call | flops 1 | bytes 1 | tf_op jit(solution)/shard_map/pallas_call | solution.py:813
  103.5 2.5 collective-permute-start.23
  106.1 3.4 %collective-permute-start.24 = (bf16[384,128]{1,0:T(8,128)(2,1)}, bf16[384,128]{1,0:T(8,128)(2,1)S(1)}, u32[]{:S(2)}, u32[]{:S(2)}) collective-permute-start(bf16[384,128]{1,0:T(8,128)(2,1)} %get-tuple-element.144), channel_id=1, source_target_pairs={{0,2},{1,3},{2,0},{3,1},{4,6},{5,7},{6,4},{7,5},{8,10},{9,11},{10,... | collective-permute-start | bytes 294920 | tf_op jit(solution)/shard_map/ppermute | solution.py:340
  109.5 3.6 %collective-permute-done.19.refs_12_ = bf16[2,96,1792]{2,1,0:T(8,128)(2,1)} collective-permute-done((bf16[2,96,1792]{2,1,0:T(8,128)(2,1)}, bf16[2,96,1792]{2,1,0:T(8,128)(2,1)}, u32[]{:S(2)}, u32[]{:S(2)}) %collective-permute-start.19) | collective-permute-done | bytes 688160 | tf_op jit(solution)/shard_map/ppermute | solution.py:340
  113.3 3.8 %collective-permute-done.24.refs_6_ = bf16[384,128]{1,0:T(8,128)(2,1)S(1)} collective-permute-done((bf16[384,128]{1,0:T(8,128)(2,1)}, bf16[384,128]{1,0:T(8,128)(2,1)S(1)}, u32[]{:S(2)}, u32[]{:S(2)}) %collective-permute-start.24) | collective-permute-done | bytes 98336 | tf_op jit(solution)/shard_map/ppermute | solution.py:340
  117.7 1.8 collective-permute-done.26.refs_16_
  121.4 18.0 %shard_map.298 = (bf16[256,768]{1,0:T(8,128)(2,1)}, bf16[9,256,768]{2,1,0:T(8,128)(2,1)}, bf16[4,256,384]{2,1,0:T(8,128)(2,1)}, bf16[4,256,384]{2,1,0:T(8,128)(2...) custom-call(s32[2]{0:T(128)} %pad_add_fusion.meta, ...), custom_call_target="tpu_custom_call" | custom-call | flops 1 | bytes 1 | tf_op jit(solution)/shard_map/pallas_call | solution.py:813
  140.0 1.6 collective-permute-start.30
  141.6 1.6 collective-permute-start.31
  143.2 1.2 collective-permute-start.32
  144.4 2.7 collective-permute-done.29.refs_1_
  148.0 1.1 copy-done
  149.1 10.0 %shard_map.299 = (bf16[2,2,96,1792]{3,2,1,0:T(8,128)(2,1)}, bf16[2,2,96,1792]{3,2,1,0:T(8,128)(2,1)}, bf16[2,2,96,1792]{3,2,1,0:T(8,128)(2,1)}, bf16[2,2,96,1792]{3,2,1,0:T(8,128)(2,1)}) custom-call(s32[2]{0:T(128)} %pad_add_fusion.meta, bf16[4,256,384]{2,1,0:T(8,128)(2,1)} %get-tuple-element.158.refs_0_, bf16[4,256,384]{2,1,0:T(8,128)(2,1)} %copy-done.30, ...), custom_call_target="tpu_custom_call" | custom-call | flops 1 | bytes 1 | tf_op jit(solution)/shard_map/pallas_call | solution.py:813
  159.7 1.5 collective-permute-start.35
  161.2 21.8 %shard_map.300 = (bf16[1152,128]{1,0:T(8,128)(2,1)}, bf16[1152,128]{1,0:T(8,128)(2,1)}, bf16[1152,128]{1,0:T(8,128)(2,1)}, bf16[1152,128]{1,0:T(8,128)(2,1)}) custom-call(s32[2]{0:T(128)} %pad_add_fusion.meta, bf16[1152,128]{1,0:T(8,128)(2,1)} %get-tuple-element.135.refs_0_, bf16[1152,128]{1,0:T(8,128)(2,1)} %copy-done.23, bf16[1152,128]{1,0:T(8,128)(2,1)} %copy-done.24, ...), custom_call_target="tpu_custom_call" | custom-call | flops 1 | bytes 1 | tf_op jit(solution)/shard_map/pallas_call | solution.py:813
  183.0 1.6 collective-permute-start.36
  184.6 1.6 collective-permute-start.37
  186.2 1.2 collective-permute-start.38
  187.4 9.8 %collective-permute-done.36 = bf16[1152,128]{1,0:T(8,128)(2,1)S(1)} collective-permute-done((bf16[1152,128]{1,0:T(8,128)(2,1)}, bf16[1152,128]{1,0:T(8,128)(2,1)S(1)}, u32[]{:S(2)}, u32[]{:S(2)}) %collective-permute-start.36) | collective-permute-done | bytes 294944 | tf_op jit(solution)/shard_map/ppermute | solution.py:340
  197.2 1.1 copy-done.15
  198.3 1.1 copy-done.16
  199.4 4.7 %shard_map.301 = (f32[2,96,1792]{2,1,0:T(8,128)}, bf16[2,96,1792]{2,1,0:T(8,128)(2,1)}, f32[2,96,1792]{2,1,0:T(8,128)}, bf16[2,96,1792]{2,1,0:T(8,128)(2,1)}) custom-call(bf16[2,2,96,1792]{3,2,1,0:T(8,128)(2,1)} %get-tuple-element.177.one_kept, bf16[2,2,96,1792]{3,2,1,0:T(8,128)(2,1)} %copy-done.15, bf16[2,2,96,1792]{3,2,1,0:T(8,128)(2,1)} %get-tuple-element.179.two_kept, ...), custom_call_target="tpu_custom_call" | custom-call | flops 1 | bytes 1 | tf_op jit(solution)/shard_map/pallas_call | solution.py:813
  204.1 4.1 %collective-permute-done.37 = bf16[1152,128]{1,0:T(8,128)(2,1)S(1)} collective-permute-done((bf16[1152,128]{1,0:T(8,128)(2,1)}, bf16[1152,128]{1,0:T(8,128)(2,1)S(1)}, u32[]{:S(2)}, u32[]{:S(2)}) %collective-permute-start.37) | collective-permute-done | bytes 294944 | tf_op jit(solution)/shard_map/ppermute | solution.py:340
  209.5 1.5 collective-permute-start.43
  212.9 6.6 %shard_map.302 = (bf16[2,2,96,576]{3,2,1,0:T(8,128)(2,1)}, bf16[2,2,96,576]{3,2,1,0:T(8,128)(2,1)}, bf16[2,2,96,576]{3,2,1,0:T(8,128)(2,1)}, bf16[2,2,96,576]{3,...) custom-call(s32[2]{0:T(128)} %pad_add_fusion.meta, ...), custom_call_target="tpu_custom_call" | custom-call | flops 1 | bytes 1 | tf_op jit(solution)/shard_map/pallas_call | solution.py:813
  219.5 1.6 collective-permute-start.40
  221.7 6.9 %shard_map.303 = (f32[256,768]{1,0:T(8,128)}, f32[16,192]{1,0:T(8,128)}, f32[16,192]{1,0:T(8,128)}, f32[16,192]{1,0:T(8,128)}, f32[16,192]{1,0:T(8,128)}) custom-call(s32[2]{0:T(128)} %pad_add_fusion.meta, bf16[256,768]{1,0:T(8,128)(2,1)} %bitcast.64, f32[256,768]{1,0:T(8,128)} %get-tuple-element.156.dmid_ref, ...), custom_call_target="tpu_custom_call" | custom-call | flops 1 | bytes 40000000 | tf_op jit(solution)/shard_map/pallas_call | solution.py:813
  229.7 3.6 %shard_map.304 = (f32[2,96,1792]{2,1,0:T(8,128)}, bf16[2,96,1792]{2,1,0:T(8,128)(2,1)}) custom-call(f32[2,96,1792]{2,1,0:T(8,128)} %get-tuple-element.211.one_kept, bf16[2,96,1792]{2,1,0:T(8,128)(2,1)} %copy-done.31, f32[2,96,1792]{2,1,0:T(8,128)} %get-tuple-element.213.two_kept, bf16[2,96,1792]{2,1,0:T(8,128)(2,1)} %copy-done.32), custom_call_target="tpu_custom_call" | custom-call | flops 1 | bytes 1 | tf_op jit(solution)/shard_map/pallas_call | solution.py:813
  233.3 5.2 %collective-permute-start.46 = (bf16[2,96,1792]{2,1,0:T(8,128)(2,1)}, bf16[2,96,1792]{2,1,0:T(8,128)(2,1)S(1)}, u32[]{:S(2)}, u32[]{:S(2)}) collective-permute-start(bf16[2,96,1792]{2,1,0:T(8,128)(2,1)} %get-tuple-element.215), channel_id=1, source_target_pairs={{0,1},{1,0},{2,3},{3,2},{4,5},{5,4},{6,7},{7,6},{8,9},{9,8},{10,11... | collective-permute-start | bytes 2064392 | tf_op jit(solution)/shard_map/ppermute | solution.py:340
  239.3 4.0 %collective-permute-start.47 = (f32[16,192]{1,0:T(8,128)S(1)}, f32[16,192]{1,0:T(8,128)S(1)}, u32[]{:S(2)}, u32[]{:S(2)}) collective-permute-start(f32[16,192]{1,0:T(8,128)S(1)} %copy-done.66), channel_id=1, source_target_pairs={{0,1},{1,0},{2,3},{3,2},{4,5},{5,4},{6,7},{7,6},{8,9},{9,8},{10,11... | collective-permute-start | bytes 36872 | tf_op jit(solution)/shard_map/ppermute | solution.py:340
  243.3 1.2 collective-permute-start.48
  244.5 1.5 collective-permute-start.49
  246.0 1.4 collective-permute-start.44
  247.4 7.1 %collective-permute-done.47 = f32[16,192]{1,0:T(8,128)S(1)} collective-permute-done((f32[16,192]{1,0:T(8,128)S(1)}, f32[16,192]{1,0:T(8,128)S(1)}, u32[]{:S(2)}, u32[]{:S(2)}) %collective-permute-start.47) | collective-permute-done | bytes 12320 | tf_op jit(solution)/shard_map/ppermute | solution.py:340
  255.2 2.1 collective-permute-done.49
  257.3 4.1 %collective-permute-done.45 = bf16[2,96,576]{2,1,0:T(8,128)(2,1)S(1)} collective-permute-done((bf16[2,96,576]{2,1,0:T(8,128)(2,1)S(1)}, bf16[2,96,576]{2,1,0:T(8,128)(2,1)S(1)}, u32[]{:S(2)}, u32[]{:S(2)}) %collective-permute-start.45) | collective-permute-done | bytes 221216 | tf_op jit(solution)/shard_map/ppermute | solution.py:340
  261.5 1.2 collective-permute-start.50
  262.9 2.2 collective-permute-start.53
  265.1 9.8 %collective-permute-done.50 = bf16[2,96,576]{2,1,0:T(8,128)(2,1)S(1)} collective-permute-done((bf16[2,96,576]{2,1,0:T(8,128)(2,1)S(1)}, bf16[2,96,576]{2,1,0:T(8,128)(2,1)S(1)}, u32[]{:S(2)}, u32[]{:S(2)}) %collective-permute-start.50) | collective-permute-done | bytes 221216 | tf_op jit(solution)/shard_map/ppermute | solution.py:340
  274.9 1.5 collective-permute-start.54
  276.5 2.2 collective-permute-done.54
  279.0 3.3 %collective-permute-done.55 = f32[16,192]{1,0:T(8,128)S(1)} collective-permute-done((f32[16,192]{1,0:T(8,128)S(1)}, f32[16,192]{1,0:T(8,128)S(1)}, u32[]{:S(2)}, u32[]{:S(2)}) %collective-permute-start.55) | collective-permute-done | bytes 12320 | tf_op jit(solution)/shard_map/ppermute | solution.py:340
  283.0 3.7 %collective-permute-done.52 = bf16[96,576]{1,0:T(8,128)(2,1)S(1)} collective-permute-done((bf16[96,576]{1,0:T(8,128)(2,1)S(1)}, bf16[96,576]{1,0:T(8,128)(2,1)S(1)}, u32[]{:S(2)}, u32[]{:S(2)}) %collective-permute-start.52) | collective-permute-done | bytes 110624 | tf_op jit(solution)/shard_map/ppermute | solution.py:340
  289.5 1.0 multiply_subtract_fusion.1
  290.5 1.0 multiply_subtract_fusion
  (237 shorter events, 32.0 us)
Async XLA Ops:
  2.6 10.0 %collective-permute-start = (bf16[96,640]{1,0:T(8,128)(2,1)S(1)}, bf16[96,640]{1,0:T(8,128)(2,1)S(1)}, u32[]{:S(2)}, u32[]{:S(2)}) collective-permute-start(bf16[96,640]{1,0:T(8,128)(2,1)S(1)} %maximum_maximum_fusion), channel_id=1, source_target_pairs={{0,2},{1,3},{2,0},{3,1},{4,6},{5,7},{6,4},{7,5},{8,10},{9,11},{10,... | collective-permute-start | bytes 368648 | tf_op jit(solution)/shard_map/ppermute | solution.py:340
  12.7 7.2 %collective-permute-start.1 = (bf16[2,96,640]{2,1,0:T(8,128)(2,1)S(1)}, bf16[2,96,640]{2,1,0:T(8,128)(2,1)S(1)}, u32[]{:S(2)}, u32[]{:S(2)}) collective-permute-start(bf16[2,96,640]{2,1,0:T(8,128)(2,1)S(1)} %pad_maximum_fusion.5), channel_id=1, source_target_pairs={{0,1},{1,0},{2,3},{3,2},{4,5},{5,4},{6,7},{7,6},{8,9},{9,8},{10,11... | collective-permute-start | bytes 737288 | tf_op jit(solution)/shard_map/ppermute | solution.py:340
  19.9 25.1 %copy-start.2 = (bf16[4,96,576]{2,1,0:T(8,128)(2,1)}, bf16[4,96,576]{2,1,0:T(8,128)(2,1)S(1)}, u32[]{:S(2)}) copy-start(bf16[4,96,576]{2,1,0:T(8,128)(2,1)S(1)} %pad_maximum_fusion.3.refs_4_) | copy-start | bytes 1327108
  20.0 11.6 %collective-permute-start.5 = (bf16[4,96,576]{2,1,0:T(8,128)(2,1)S(1)}, bf16[4,96,576]{2,1,0:T(8,128)(2,1)S(1)}, u32[]{:S(2)}, u32[]{:S(2)}) collective-permute-start(bf16[4,96,576]{2,1,0:T(8,128)(2,1)S(1)} %pad_maximum_fusion.3.refs_4_), channel_id=1, source_target_pairs={{0,16},{4,20},{8,24},{12,28},{16,0},{20,4},{24,8},{28,12},{1,17},{... | collective-permute-start | bytes 1327112 | tf_op jit(solution)/shard_map/ppermute | solution.py:340
  21.3 12.1 %collective-permute-start.3 = (bf16[4,96,576]{2,1,0:T(8,128)(2,1)S(1)}, bf16[4,96,576]{2,1,0:T(8,128)(2,1)S(1)}, u32[]{:S(2)}, u32[]{:S(2)}) collective-permute-start(bf16[4,96,576]{2,1,0:T(8,128)(2,1)S(1)} %pad_maximum_fusion.3.refs_4_), channel_id=1, source_target_pairs={{0,8},{4,12},{8,0},{12,4},{16,24},{20,28},{24,16},{28,20},{1,9},{5... | collective-permute-start | bytes 1327112 | tf_op jit(solution)/shard_map/ppermute | solution.py:340
  25.4 17.9 %collective-permute-start.2 = (bf16[96,1792]{1,0:T(8,128)(2,1)S(1)}, bf16[96,1792]{1,0:T(8,128)(2,1)S(1)}, u32[]{:S(2)}, u32[]{:S(2)}) collective-permute-start(bf16[96,1792]{1,0:T(8,128)(2,1)S(1)} %concatenate.23), channel_id=1, source_target_pairs={{0,2},{1,3},{2,0},{3,1},{4,6},{5,7},{6,4},{7,5},{8,10},{9,11},{10,... | collective-permute-start | bytes 1032200 | tf_op jit(solution)/shard_map/ppermute | solution.py:340
  31.5 11.8 %collective-permute-start.6 = (bf16[2,96,576]{2,1,0:T(8,128)(2,1)S(1)}, bf16[2,96,576]{2,1,0:T(8,128)(2,1)S(1)}, u32[]{:S(2)}, u32[]{:S(2)}) collective-permute-start(bf16[2,96,576]{2,1,0:T(8,128)(2,1)S(1)} %slice.126), channel_id=1, source_target_pairs={{0,8},{4,12},{8,0},{12,4},{16,24},{20,28},{24,16},{28,20},{1,9},{5... | collective-permute-start | bytes 663560 | tf_op jit(solution)/shard_map/ppermute | solution.py:340
  33.4 9.9 %collective-permute-start.4 = (bf16[2,96,576]{2,1,0:T(8,128)(2,1)S(1)}, bf16[2,96,576]{2,1,0:T(8,128)(2,1)}, u32[]{:S(2)}, u32[]{:S(2)}) collective-permute-start(bf16[2,96,576]{2,1,0:T(8,128)(2,1)S(1)} %slice.125), channel_id=1, source_target_pairs={{0,16},{4,20},{8,24},{12,28},{16,0},{20,4},{24,8},{28,12},{1,17},{... | collective-permute-start | bytes 663560 | tf_op jit(solution)/shard_map/ppermute | solution.py:340
  44.3 16.7 %collective-permute-start.7 = (bf16[2,96,1792]{2,1,0:T(8,128)(2,1)}, bf16[2,96,1792]{2,1,0:T(8,128)(2,1)}, u32[]{:S(2)}, u32[]{:S(2)}) collective-permute-start(bf16[2,96,1792]{2,1,0:T(8,128)(2,1)} %pad_maximum_fusion.2), channel_id=1, source_target_pairs={{0,1},{1,0},{2,3},{3,2},{4,5},{5,4},{6,7},{7,6},{8,9},{9,8},{10,11... | collective-permute-start | bytes 2064392 | tf_op jit(solution)/shard_map/ppermute | solution.py:340
  45.0 1.9 collective-permute-start.8
  45.0 2.9 collective-permute-start.10
  45.5 3.5 %collective-permute-start.9 = (bf16[4,96,576]{2,1,0:T(8,128)(2,1)S(1)}, bf16[4,96,576]{2,1,0:T(8,128)(2,1)S(1)}, u32[]{:S(2)}, u32[]{:S(2)}) collective-permute-start(bf16[4,96,576]{2,1,0:T(8,128)(2,1)S(1)} %collective-permute-done.3.refs_5_), channel_id=1, source_target_pairs={{0,4},{4,0},{8,12},{12,8},{16,20},{20,16},{24,28},{28,24},{1,5},{5... | collective-permute-start | bytes 1327112 | tf_op jit(solution)/shard_map/ppermute | solution.py:340
  45.5 2.7 collective-permute-start.11
  46.9 2.1 collective-permute-start.12
  62.4 33.0 %copy-start.1 = (bf16[4,96,1792]{2,1,0:T(8,128)(2,1)}, bf16[4,96,1792]{2,1,0:T(8,128)(2,1)S(1)}, u32[]{:S(2)}) copy-start(bf16[4,96,1792]{2,1,0:T(8,128)(2,1)S(1)} %pad_maximum_fusion.refs_8_) | copy-start | bytes 4128772
  62.4 30.4 %collective-permute-start.17 = (bf16[4,96,1792]{2,1,0:T(8,128)(2,1)S(1)}, bf16[4,96,1792]{2,1,0:T(8,128)(2,1)S(1)}, u32[]{:S(2)}, u32[]{:S(2)}) collective-permute-start(bf16[4,96,1792]{2,1,0:T(8,128)(2,1)S(1)} %pad_maximum_fusion.refs_8_), channel_id=1, source_target_pairs={{0,16},{4,20},{8,24},{12,28},{16,0},{20,4},{24,8},{28,12},{1,17},{... | collective-permute-start | bytes 4128776 | tf_op jit(solution)/shard_map/ppermute | solution.py:340
  63.0 30.0 %collective-permute-start.16 = (bf16[4,96,1792]{2,1,0:T(8,128)(2,1)S(1)}, bf16[4,96,1792]{2,1,0:T(8,128)(2,1)S(1)}, u32[]{:S(2)}, u32[]{:S(2)}) collective-permute-start(bf16[4,96,1792]{2,1,0:T(8,128)(2,1)S(1)} %pad_maximum_fusion.refs_8_), channel_id=1, source_target_pairs={{0,8},{4,12},{8,0},{12,4},{16,24},{20,28},{24,16},{28,20},{1,9},{5... | collective-permute-start | bytes 4128776 | tf_op jit(solution)/shard_map/ppermute | solution.py:340
  63.5 12.3 %collective-permute-start.13 = (bf16[1152,128]{1,0:T(8,128)(2,1)S(1)}, bf16[1152,128]{1,0:T(8,128)(2,1)S(1)}, u32[]{:S(2)}, u32[]{:S(2)}) collective-permute-start(bf16[1152,128]{1,0:T(8,128)(2,1)S(1)} %copy-done.63), channel_id=1, source_target_pairs={{0,1},{1,0},{2,3},{3,2},{4,5},{5,4},{6,7},{7,6},{8,9},{9,8},{10,11... | collective-permute-start | bytes 884744 | tf_op jit(solution)/shard_map/ppermute | solution.py:340
  65.1 23.9 %collective-permute-start.14 = (bf16[1152,128]{1,0:T(8,128)(2,1)S(1)}, bf16[1152,128]{1,0:T(8,128)(2,1)S(1)}, u32[]{:S(2)}, u32[]{:S(2)}) collective-permute-start(bf16[1152,128]{1,0:T(8,128)(2,1)S(1)} %copy-done.62), channel_id=1, source_target_pairs={{0,2},{1,3},{2,0},{3,1},{4,6},{5,7},{6,4},{7,5},{8,10},{9,11},{10,... | collective-permute-start | bytes 884744 | tf_op jit(solution)/shard_map/ppermute | solution.py:340
  68.5 20.6 %collective-permute-start.15 = (bf16[1152,128]{1,0:T(8,128)(2,1)S(1)}, bf16[1152,128]{1,0:T(8,128)(2,1)S(1)}, u32[]{:S(2)}, u32[]{:S(2)}) collective-permute-start(bf16[1152,128]{1,0:T(8,128)(2,1)S(1)} %copy-done.61), channel_id=1, source_target_pairs={{0,3},{1,2},{2,1},{3,0},{4,7},{5,6},{6,5},{7,4},{8,11},{9,10},{10,... | collective-permute-start | bytes 884744 | tf_op jit(solution)/shard_map/ppermute | solution.py:340
  75.9 27.6 %collective-permute-start.20 = (bf16[4,96,1792]{2,1,0:T(8,128)(2,1)S(1)}, bf16[4,96,1792]{2,1,0:T(8,128)(2,1)S(1)}, u32[]{:S(2)}, u32[]{:S(2)}) collective-permute-start(bf16[4,96,1792]{2,1,0:T(8,128)(2,1)S(1)} %pad_maximum_fusion.refs_8_), channel_id=1, source_target_pairs={{0,4},{4,0},{8,12},{12,8},{16,20},{20,16},{24,28},{28,24},{1,5},{5... | collective-permute-start | bytes 4128776 | tf_op jit(solution)/shard_map/ppermute | solution.py:340
  93.0 27.6 %copy-start.5 = (bf16[4,96,1792]{2,1,0:T(8,128)(2,1)}, bf16[4,96,1792]{2,1,0:T(8,128)(2,1)S(1)}, u32[]{:S(2)}) copy-start(bf16[4,96,1792]{2,1,0:T(8,128)(2,1)S(1)} %collective-permute-done.16.refs_9_) | copy-start | bytes 4128772
  93.0 10.5 %collective-permute-start.21 = (bf16[4,96,1792]{2,1,0:T(8,128)(2,1)S(1)}, bf16[4,96,1792]{2,1,0:T(8,128)(2,1)S(1)}, u32[]{:S(2)}, u32[]{:S(2)}) collective-permute-start(bf16[4,96,1792]{2,1,0:T(8,128)(2,1)S(1)} %collective-permute-done.16.refs_9_), channel_id=1, source_target_pairs={{0,4},{4,0},{8,12},{12,8},{16,20},{20,16},{24,28},{28,24},{1,5},{5... | collective-permute-start | bytes 4128776 | tf_op jit(solution)/shard_map/ppermute | solution.py:340
  93.0 10.5 %collective-permute-start.22 = (bf16[4,96,1792]{2,1,0:T(8,128)(2,1)S(1)}, bf16[4,96,1792]{2,1,0:T(8,128)(2,1)S(1)}, u32[]{:S(2)}, u32[]{:S(2)}) collective-permute-start(bf16[4,96,1792]{2,1,0:T(8,128)(2,1)S(1)} %collective-permute-done.17.refs_10_), channel_id=1, source_target_pairs={{0,4},{4,0},{8,12},{12,8},{16,20},{20,16},{24,28},{28,24},{1,5},{5... | collective-permute-start | bytes 4128776 | tf_op jit(solution)/shard_map/ppermute | solution.py:340
  95.4 17.6 %collective-permute-start.19 = (bf16[2,96,1792]{2,1,0:T(8,128)(2,1)}, bf16[2,96,1792]{2,1,0:T(8,128)(2,1)}, u32[]{:S(2)}, u32[]{:S(2)}) collective-permute-start(bf16[2,96,1792]{2,1,0:T(8,128)(2,1)} %slice.104), channel_id=1, source_target_pairs={{0,8},{4,12},{8,0},{12,4},{16,24},{20,28},{24,16},{28,20},{1,9},{5... | collective-permute-start | bytes 2064392 | tf_op jit(solution)/shard_map/ppermute | solution.py:340
  95.9 17.3 %collective-permute-start.18 = (bf16[2,96,1792]{2,1,0:T(8,128)(2,1)}, bf16[2,96,1792]{2,1,0:T(8,128)(2,1)}, u32[]{:S(2)}, u32[]{:S(2)}) collective-permute-start(bf16[2,96,1792]{2,1,0:T(8,128)(2,1)} %slice.103), channel_id=1, source_target_pairs={{0,16},{4,20},{8,24},{12,28},{16,0},{20,4},{24,8},{28,12},{1,17},{... | collective-permute-start | bytes 2064392 | tf_op jit(solution)/shard_map/ppermute | solution.py:340
  103.5 9.8 %collective-permute-start.23 = (bf16[384,128]{1,0:T(8,128)(2,1)}, bf16[384,128]{1,0:T(8,128)(2,1)S(1)}, u32[]{:S(2)}, u32[]{:S(2)}) collective-permute-start(bf16[384,128]{1,0:T(8,128)(2,1)} %get-tuple-element.143), channel_id=1, source_target_pairs={{0,1},{1,0},{2,3},{3,2},{4,5},{5,4},{6,7},{7,6},{8,9},{9,8},{10,11... | collective-permute-start | bytes 294920 | tf_op jit(solution)/shard_map/ppermute | solution.py:340
  106.1 11.1 %collective-permute-start.24 = (bf16[384,128]{1,0:T(8,128)(2,1)}, bf16[384,128]{1,0:T(8,128)(2,1)S(1)}, u32[]{:S(2)}, u32[]{:S(2)}) collective-permute-start(bf16[384,128]{1,0:T(8,128)(2,1)} %get-tuple-element.144), channel_id=1, source_target_pairs={{0,2},{1,3},{2,0},{3,1},{4,6},{5,7},{6,4},{7,5},{8,10},{9,11},{10,... | collective-permute-start | bytes 294920 | tf_op jit(solution)/shard_map/ppermute | solution.py:340
  109.4 7.7 %collective-permute-start.25 = (bf16[384,128]{1,0:T(8,128)(2,1)}, bf16[384,128]{1,0:T(8,128)(2,1)S(1)}, u32[]{:S(2)}, u32[]{:S(2)}) collective-permute-start(bf16[384,128]{1,0:T(8,128)(2,1)} %get-tuple-element.145), channel_id=1, source_target_pairs={{0,3},{1,2},{2,1},{3,0},{4,7},{5,6},{6,5},{7,4},{8,11},{9,10},{10,... | collective-permute-start | bytes 294920 | tf_op jit(solution)/shard_map/ppermute | solution.py:340
  117.1 2.4 collective-permute-start.26
  117.2 3.3 %collective-permute-start.27 = (bf16[2,96,1792]{2,1,0:T(8,128)(2,1)}, bf16[2,96,1792]{2,1,0:T(8,128)(2,1)S(1)}, u32[]{:S(2)}, u32[]{:S(2)}) collective-permute-start(bf16[2,96,1792]{2,1,0:T(8,128)(2,1)} %collective-permute-done.19.refs_12_), channel_id=1, source_target_pairs={{0,4},{4,0},{8,12},{12,8},{16,20},{20,16},{24,28},{28,24},{1,5},{5... | collective-permute-start | bytes 2064392 | tf_op jit(solution)/shard_map/ppermute | solution.py:340
  139.4 7.6 %collective-permute-start.28 = (bf16[9,256,768]{2,1,0:T(8,128)(2,1)}, bf16[9,256,768]{2,1,0:T(8,128)(2,1)S(1)}, u32[]{:S(2)}, u32[]{:S(2)}) collective-permute-start(bf16[9,256,768]{2,1,0:T(8,128)(2,1)} %get-tuple-element.157.refs_2_.refs_0_), channel_id=1, source_target_pairs={{0,4},{4,0},{8,12},{12,8},{16,20},{20,16},{24,28},{28,24},{1,5},{5... | collective-permute-start | bytes 10616840 | tf_op jit(solution)/shard_map/ppermute | solution.py:340
  139.6 7.4 %collective-permute-start.29 = (bf16[4,256,384]{2,1,0:T(8,128)(2,1)}, bf16[4,256,384]{2,1,0:T(8,128)(2,1)S(1)}, u32[]{:S(2)}, u32[]{:S(2)}) collective-permute-start(bf16[4,256,384]{2,1,0:T(8,128)(2,1)} %get-tuple-element.159), channel_id=1, source_target_pairs={{0,4},{4,0},{8,12},{12,8},{16,20},{20,16},{24,28},{28,24},{1,5},{5... | collective-permute-start | bytes 2359304 | tf_op jit(solution)/shard_map/ppermute | solution.py:340
  140.0 19.0 %collective-permute-start.30 = (bf16[384,128]{1,0:T(8,128)(2,1)}, bf16[384,128]{1,0:T(8,128)(2,1)S(1)}, u32[]{:S(2)}, u32[]{:S(2)}) collective-permute-start(bf16[384,128]{1,0:T(8,128)(2,1)} %get-tuple-element.165), channel_id=1, source_target_pairs={{0,1},{1,0},{2,3},{3,2},{4,5},{5,4},{6,7},{7,6},{8,9},{9,8},{10,11... | collective-permute-start | bytes 294920 | tf_op jit(solution)/shard_map/ppermute | solution.py:340
  141.6 17.5 %collective-permute-start.31 = (bf16[384,128]{1,0:T(8,128)(2,1)}, bf16[384,128]{1,0:T(8,128)(2,1)S(1)}, u32[]{:S(2)}, u32[]{:S(2)}) collective-permute-start(bf16[384,128]{1,0:T(8,128)(2,1)} %get-tuple-element.166), channel_id=1, source_target_pairs={{0,2},{1,3},{2,0},{3,1},{4,6},{5,7},{6,4},{7,5},{8,10},{9,11},{10,... | collective-permute-start | bytes 294920 | tf_op jit(solution)/shard_map/ppermute | solution.py:340
  143.2 15.9 %collective-permute-start.32 = (bf16[384,128]{1,0:T(8,128)(2,1)}, bf16[384,128]{1,0:T(8,128)(2,1)S(1)}, u32[]{:S(2)}, u32[]{:S(2)}) collective-permute-start(bf16[384,128]{1,0:T(8,128)(2,1)} %get-tuple-element.167), channel_id=1, source_target_pairs={{0,3},{1,2},{2,1},{3,0},{4,7},{5,6},{6,5},{7,4},{8,11},{9,10},{10,... | collective-permute-start | bytes 294920 | tf_op jit(solution)/shard_map/ppermute | solution.py:340
  159.1 38.1 %collective-permute-start.34 = (bf16[2,2,96,1792]{3,2,1,0:T(8,128)(2,1)}, bf16[2,2,96,1792]{3,2,1,0:T(8,128)(2,1)S(1)}, u32[]{:S(2)}, u32[]{:S(2)}) collective-permute-start(bf16[2,2,96,1792]{3,2,1,0:T(8,128)(2,1)} %get-tuple-element.173), channel_id=1, source_target_pairs={{0,16},{4,20},{8,24},{12,28},{16,0},{20,4},{24,8},{28,12},{1,17},{... | collective-permute-start | bytes 4128776 | tf_op jit(solution)/shard_map/ppermute | solution.py:340
  159.7 37.5 %collective-permute-start.35 = (bf16[2,2,96,1792]{3,2,1,0:T(8,128)(2,1)}, bf16[2,2,96,1792]{3,2,1,0:T(8,128)(2,1)S(1)}, u32[]{:S(2)}, u32[]{:S(2)}) collective-permute-start(bf16[2,2,96,1792]{3,2,1,0:T(8,128)(2,1)} %get-tuple-element.174), channel_id=1, source_target_pairs={{0,8},{4,12},{8,0},{12,4},{16,24},{20,28},{24,16},{28,20},{1,9},{5... | collective-permute-start | bytes 4128776 | tf_op jit(solution)/shard_map/ppermute | solution.py:340
  183.0 14.2 %collective-permute-start.36 = (bf16[1152,128]{1,0:T(8,128)(2,1)}, bf16[1152,128]{1,0:T(8,128)(2,1)S(1)}, u32[]{:S(2)}, u32[]{:S(2)}) collective-permute-start(bf16[1152,128]{1,0:T(8,128)(2,1)} %get-tuple-element.175), channel_id=1, source_target_pairs={{0,1},{1,0},{2,3},{3,2},{4,5},{5,4},{6,7},{7,6},{8,9},{9,8},{10,11... | collective-permute-start | bytes 884744 | tf_op jit(solution)/shard_map/ppermute | solution.py:340
  184.6 23.7 %collective-permute-start.37 = (bf16[1152,128]{1,0:T(8,128)(2,1)}, bf16[1152,128]{1,0:T(8,128)(2,1)S(1)}, u32[]{:S(2)}, u32[]{:S(2)}) collective-permute-start(bf16[1152,128]{1,0:T(8,128)(2,1)} %get-tuple-element.182), channel_id=1, source_target_pairs={{0,2},{1,3},{2,0},{3,1},{4,6},{5,7},{6,4},{7,5},{8,10},{9,11},{10,... | collective-permute-start | bytes 884744 | tf_op jit(solution)/shard_map/ppermute | solution.py:340
  186.2 22.1 %collective-permute-start.38 = (bf16[1152,128]{1,0:T(8,128)(2,1)}, bf16[1152,128]{1,0:T(8,128)(2,1)S(1)}, u32[]{:S(2)}, u32[]{:S(2)}) collective-permute-start(bf16[1152,128]{1,0:T(8,128)(2,1)} %get-tuple-element.183), channel_id=1, source_target_pairs={{0,3},{1,2},{2,1},{3,0},{4,7},{5,6},{6,5},{7,4},{8,11},{9,10},{10,... | collective-permute-start | bytes 884744 | tf_op jit(solution)/shard_map/ppermute | solution.py:340
  208.4 2.9 %collective-permute-start.39 = (bf16[3,1152,128]{2,1,0:T(8,128)(2,1)S(1)}, bf16[3,1152,128]{2,1,0:T(8,128)(2,1)S(1)}, u32[]{:S(2)}, u32[]{:S(2)}) collective-permute-start(bf16[3,1152,128]{2,1,0:T(8,128)(2,1)S(1)} %pad_maximum_fusion.1.refs_4_), channel_id=1, source_target_pairs={{0,4},{4,0},{8,12},{12,8},{16,20},{20,16},{24,28},{28,24},{1,5},{5... | collective-permute-start | bytes 2654216 | tf_op jit(solution)/shard_map/ppermute | solution.py:340
  208.5 2.8 collective-permute-start.33
  209.0 19.6 %collective-permute-start.42 = (bf16[2,96,1792]{2,1,0:T(8,128)(2,1)S(1)}, bf16[2,96,1792]{2,1,0:T(8,128)(2,1)S(1)}, u32[]{:S(2)}, u32[]{:S(2)}) collective-permute-start(bf16[2,96,1792]{2,1,0:T(8,128)(2,1)S(1)} %copy-done.60), channel_id=1, source_target_pairs={{0,8},{4,12},{8,0},{12,4},{16,24},{20,28},{24,16},{28,20},{1,9},{5... | collective-permute-start | bytes 2064392 | tf_op jit(solution)/shard_map/ppermute | solution.py:340
  209.5 19.1 %collective-permute-start.43 = (bf16[2,96,1792]{2,1,0:T(8,128)(2,1)S(1)}, bf16[2,96,1792]{2,1,0:T(8,128)(2,1)S(1)}, u32[]{:S(2)}, u32[]{:S(2)}) collective-permute-start(bf16[2,96,1792]{2,1,0:T(8,128)(2,1)S(1)} %copy-done.59), channel_id=1, source_target_pairs={{0,16},{4,20},{8,24},{12,28},{16,0},{20,4},{24,8},{28,12},{1,17},{... | collective-permute-start | bytes 2064392 | tf_op jit(solution)/shard_map/ppermute | solution.py:340
  219.5 18.9 %collective-permute-start.40 = (bf16[2,2,96,576]{3,2,1,0:T(8,128)(2,1)}, bf16[2,2,96,576]{3,2,1,0:T(8,128)(2,1)S(1)}, u32[]{:S(2)}, u32[]{:S(2)}) collective-permute-start(bf16[2,2,96,576]{3,2,1,0:T(8,128)(2,1)} %get-tuple-element.196), channel_id=1, source_target_pairs={{0,16},{4,20},{8,24},{12,28},{16,0},{20,4},{24,8},{28,12},{1,17},{... | collective-permute-start | bytes 1327112 | tf_op jit(solution)/shard_map/ppermute | solution.py:340
  221.1 17.5 %collective-permute-start.41 = (bf16[2,2,96,576]{3,2,1,0:T(8,128)(2,1)}, bf16[2,2,96,576]{3,2,1,0:T(8,128)(2,1)S(1)}, u32[]{:S(2)}, u32[]{:S(2)}) collective-permute-start(bf16[2,2,96,576]{3,2,1,0:T(8,128)(2,1)} %get-tuple-element.198), channel_id=1, source_target_pairs={{0,8},{4,12},{8,0},{12,4},{16,24},{20,28},{24,16},{28,20},{1,9},{5... | collective-permute-start | bytes 1327112 | tf_op jit(solution)/shard_map/ppermute | solution.py:340
  233.3 28.1 %collective-permute-start.46 = (bf16[2,96,1792]{2,1,0:T(8,128)(2,1)}, bf16[2,96,1792]{2,1,0:T(8,128)(2,1)S(1)}, u32[]{:S(2)}, u32[]{:S(2)}) collective-permute-start(bf16[2,96,1792]{2,1,0:T(8,128)(2,1)} %get-tuple-element.215), channel_id=1, source_target_pairs={{0,1},{1,0},{2,3},{3,2},{4,5},{5,4},{6,7},{7,6},{8,9},{9,8},{10,11... | collective-permute-start | bytes 2064392 | tf_op jit(solution)/shard_map/ppermute | solution.py:340
  238.8 23.9 %copy-start.14 = (f32[2,96,1792]{2,1,0:T(8,128)S(1)}, f32[2,96,1792]{2,1,0:T(8,128)}, u32[]{:S(2)}) copy-start(f32[2,96,1792]{2,1,0:T(8,128)} %get-tuple-element.224) | copy-start | bytes 4128772
  239.3 15.2 %collective-permute-start.47 = (f32[16,192]{1,0:T(8,128)S(1)}, f32[16,192]{1,0:T(8,128)S(1)}, u32[]{:S(2)}, u32[]{:S(2)}) collective-permute-start(f32[16,192]{1,0:T(8,128)S(1)} %copy-done.66), channel_id=1, source_target_pairs={{0,1},{1,0},{2,3},{3,2},{4,5},{5,4},{6,7},{7,6},{8,9},{9,8},{10,11... | collective-permute-start | bytes 36872 | tf_op jit(solution)/shard_map/ppermute | solution.py:340
  243.3 11.8 %collective-permute-start.48 = (f32[16,192]{1,0:T(8,128)S(1)}, f32[16,192]{1,0:T(8,128)S(1)}, u32[]{:S(2)}, u32[]{:S(2)}) collective-permute-start(f32[16,192]{1,0:T(8,128)S(1)} %copy-done.65), channel_id=1, source_target_pairs={{0,2},{1,3},{2,0},{3,1},{4,6},{5,7},{6,4},{7,5},{8,10},{9,11},{10,... | collective-permute-start | bytes 36872 | tf_op jit(solution)/shard_map/ppermute | solution.py:340
  244.5 12.8 %collective-permute-start.49 = (f32[16,192]{1,0:T(8,128)S(1)}, f32[16,192]{1,0:T(8,128)S(1)}, u32[]{:S(2)}, u32[]{:S(2)}) collective-permute-start(f32[16,192]{1,0:T(8,128)S(1)} %copy-done.64), channel_id=1, source_target_pairs={{0,3},{1,2},{2,1},{3,0},{4,7},{5,6},{6,5},{7,4},{8,11},{9,10},{10,... | collective-permute-start | bytes 36872 | tf_op jit(solution)/shard_map/ppermute | solution.py:340
  246.0 11.3 %collective-permute-start.44 = (bf16[2,96,576]{2,1,0:T(8,128)(2,1)S(1)}, bf16[2,96,576]{2,1,0:T(8,128)(2,1)S(1)}, u32[]{:S(2)}, u32[]{:S(2)}) collective-permute-start(bf16[2,96,576]{2,1,0:T(8,128)(2,1)S(1)} %fusion.9), channel_id=1, source_target_pairs={{0,8},{4,12},{8,0},{12,4},{16,24},{20,28},{24,16},{28,20},{1,9},{5... | collective-permute-start | bytes 663560 | tf_op jit(solution)/shard_map/ppermute | solution.py:340
  254.6 6.8 %collective-permute-start.45 = (bf16[2,96,576]{2,1,0:T(8,128)(2,1)S(1)}, bf16[2,96,576]{2,1,0:T(8,128)(2,1)S(1)}, u32[]{:S(2)}, u32[]{:S(2)}) collective-permute-start(bf16[2,96,576]{2,1,0:T(8,128)(2,1)S(1)} %fusion.10), channel_id=1, source_target_pairs={{0,16},{4,20},{8,24},{12,28},{16,0},{20,4},{24,8},{28,12},{1,17},{... | collective-permute-start | bytes 663560 | tf_op jit(solution)/shard_map/ppermute | solution.py:340
  261.4 3.7 %collective-permute-start.51 = (f32[16,192]{1,0:T(8,128)S(1)}, f32[16,192]{1,0:T(8,128)S(1)}, u32[]{:S(2)}, u32[]{:S(2)}) collective-permute-start(f32[16,192]{1,0:T(8,128)S(1)} %add_add_fusion), channel_id=1, source_target_pairs={{0,4},{4,0},{8,12},{12,8},{16,20},{20,16},{24,28},{28,24},{1,5},{5... | collective-permute-start | bytes 36872 | tf_op jit(solution)/shard_map/ppermute | solution.py:340
  261.5 13.4 %collective-permute-start.50 = (bf16[2,96,576]{2,1,0:T(8,128)(2,1)S(1)}, bf16[2,96,576]{2,1,0:T(8,128)(2,1)S(1)}, u32[]{:S(2)}, u32[]{:S(2)}) collective-permute-start(bf16[2,96,576]{2,1,0:T(8,128)(2,1)S(1)} %fusion.2), channel_id=1, source_target_pairs={{0,1},{1,0},{2,3},{3,2},{4,5},{5,4},{6,7},{7,6},{8,9},{9,8},{10,11... | collective-permute-start | bytes 663560 | tf_op jit(solution)/shard_map/ppermute | solution.py:340
  262.8 19.6 %copy-start.55 = (f32[12,192]{1,0:T(8,128)S(1)}, f32[12,192]{1,0:T(8,128)}, u32[]{:S(2)}) copy-start(f32[12,192]{1,0:T(8,128)} %param.23) | copy-start | bytes 27652
  262.9 23.9 %copy-start.26 = (f32[96,576]{1,0:T(8,128)S(1)}, f32[96,576]{1,0:T(8,128)}, u32[]{:S(2)}) copy-start(f32[96,576]{1,0:T(8,128)} %param.19) | copy-start | bytes 663556
  262.9 23.9 %copy-start.45 = (f32[96,576]{1,0:T(8,128)S(1)}, f32[96,576]{1,0:T(8,128)}, u32[]{:S(2)}) copy-start(f32[96,576]{1,0:T(8,128)} %param.25) | copy-start | bytes 663556
  262.9 23.9 %copy-start.46 = (f32[96,576]{1,0:T(8,128)S(1)}, f32[96,576]{1,0:T(8,128)}, u32[]{:S(2)}) copy-start(f32[96,576]{1,0:T(8,128)} %param.24) | copy-start | bytes 663556
  262.9 24.8 %collective-permute-start.53 = (bf16[96,1792]{1,0:T(8,128)(2,1)S(1)}, bf16[96,1792]{1,0:T(8,128)(2,1)S(1)}, u32[]{:S(2)}, u32[]{:S(2)}) collective-permute-start(bf16[96,1792]{1,0:T(8,128)(2,1)S(1)} %fusion.5), channel_id=1, source_target_pairs={{0,2},{1,3},{2,0},{3,1},{4,6},{5,7},{6,4},{7,5},{8,10},{9,11},{10,... | collective-permute-start | bytes 1032200 | tf_op jit(solution)/shard_map/ppermute | solution.py:340
  274.9 3.7 %collective-permute-start.54 = (f32[16,192]{1,0:T(8,128)S(1)}, f32[16,192]{1,0:T(8,128)S(1)}, u32[]{:S(2)}, u32[]{:S(2)}) collective-permute-start(f32[16,192]{1,0:T(8,128)S(1)} %add.126), channel_id=1, source_target_pairs={{0,8},{4,12},{8,0},{12,4},{16,24},{20,28},{24,16},{28,20},{1,9},{5... | collective-permute-start | bytes 36872 | tf_op jit(solution)/shard_map/ppermute | solution.py:340
  278.6 3.7 %collective-permute-start.55 = (f32[16,192]{1,0:T(8,128)S(1)}, f32[16,192]{1,0:T(8,128)S(1)}, u32[]{:S(2)}, u32[]{:S(2)}) collective-permute-start(f32[16,192]{1,0:T(8,128)S(1)} %add.151), channel_id=1, source_target_pairs={{0,16},{4,20},{8,24},{12,28},{16,0},{20,4},{24,8},{28,12},{1,17},{... | collective-permute-start | bytes 36872 | tf_op jit(solution)/shard_map/ppermute | solution.py:340
  279.0 7.8 %collective-permute-start.52 = (bf16[96,576]{1,0:T(8,128)(2,1)S(1)}, bf16[96,576]{1,0:T(8,128)(2,1)S(1)}, u32[]{:S(2)}, u32[]{:S(2)}) collective-permute-start(bf16[96,576]{1,0:T(8,128)(2,1)S(1)} %fusion.12), channel_id=1, source_target_pairs={{0,2},{1,3},{2,0},{3,1},{4,6},{5,7},{6,4},{7,5},{8,10},{9,11},{10,... | collective-permute-start | bytes 331784 | tf_op jit(solution)/shard_map/ppermute | solution.py:340
  (59 other events, 334.8 us)
